TPU v7x, 32 devices: a whole 2x2x4 slice. The times are simulated.
32 devices in a mesh: depth: 2 (over x), row: 4 (over y, core), col: 4 (over z).
Axes of the slice: x: 2, y: 2, z: 4, core: 2. Of those that a mesh axis runs over, the one named last changes fastest.
Arguments:
- x_out: float32 [8192, 768], P(('depth', 'col'), 'row'), may hold values from -6 to 6
- v_out: float32 [8192, 768], P(('depth', 'col'), 'row'), may hold values from -6 to 6
- dx_out: float32 [8192, 768], P(('depth', 'col'), 'row'), may hold values from -6 to 6
- dv_out: float32 [8192, 768], P(('depth', 'col'), 'row'), may hold values from -6 to 6
- gate_weight: bfloat16 [14336, 8192], P(('col', 'row'), 'depth'), may hold values from -0.0625 to 0.0625
- up_weight: bfloat16 [14336, 8192], P(('col', 'row'), 'depth'), may hold values from -0.0625 to 0.0625
- down_weight: bfloat16 [14336, 8192], P(('col', 'row'), 'depth'), may hold values from -0.046875 to 0.046875
Outputs:
- x_prev: float32 [8192, 768], P(('depth', 'col'), 'row')
- v_prev: float32 [8192, 768], P(('depth', 'col'), 'row')
- dx_prev: float32 [8192, 768], P(('depth', 'col'), 'row')
- grad_gate: float32 [14336, 8192], P(('col', 'row'), 'depth')
- grad_up: float32 [14336, 8192], P(('col', 'row'), 'depth')
- grad_down: float32 [14336, 8192], P(('col', 'row'), 'depth')
All inputs are finite; a program needn't handle non-finite values.
Results may differ from a plain program's by a relative error of at most 0.0061.
Values may be sent and summed in bfloat16 or wider, within the bound.
A program may use at most 256 MiB of HBM per device.

v0:
```python
import jax
import jax.numpy as jnp
from jax import lax
from jax.sharding import PartitionSpec as P

momentum = 0.5


def contract(left, right, left_dim, right_dim):
    return lax.dot_general(
        left, right, (((left_dim,), (right_dim,)), ((), ())), preferred_element_type=jnp.float32
    )


def reduce_hidden(term_fn, count_rows):
    return lax.psum_scatter(
        term_fn(jnp.int32(0), count_rows * lax.axis_size("col")),
        "col",
        scatter_dimension=0,
        tiled=True,
    )


def nonlinear(gate, up_val, d_act):
    sig = jax.nn.sigmoid(gate)
    act = (gate * sig * up_val).astype(jnp.bfloat16)
    d_gate = (d_act * up_val * sig * (1.0 + gate * (1.0 - sig))).astype(jnp.bfloat16)
    d_up = (d_act * gate * sig).astype(jnp.bfloat16)
    return (act, d_gate, d_up)


def on_device(x_out, v_out, dx_out, dv_out, gate_weight, up_weight, down_weight):
    x_prev = x_out - v_out
    x_half = x_prev.astype(jnp.bfloat16)
    df_half = ((1.0 - momentum) * (dx_out + dv_out)).astype(jnp.bfloat16)
    x_cols, df_cols = (
        lax.all_gather(x_half, "col", axis=0, tiled=True),
        lax.all_gather(df_half, "col", axis=0, tiled=True),
    )
    gate_full, up_full, down_full, x_all, df_all = (
        lax.all_gather(gate_weight, "row", axis=0, tiled=True),
        lax.all_gather(up_weight, "row", axis=0, tiled=True),
        lax.all_gather(down_weight, "row", axis=0, tiled=True),
        lax.all_gather(x_cols, "row", axis=1, tiled=True),
        lax.all_gather(df_cols, "row", axis=1, tiled=True),
    )
    gate_part = contract(gate_full, x_cols, 1, 0)
    up_part = contract(up_full, x_cols, 1, 0)
    dact_part = contract(down_full, df_cols, 1, 0)
    gate, up_val, d_act = lax.psum((gate_part, up_part, dact_part), "depth")
    act, d_gate, d_up = nonlinear(gate, up_val, d_act)
    count_rows = x_out.shape[0]

    def down_term(start, count):
        return contract(down_full, act, 0, 0)

    y_out = reduce_hidden(down_term, count_rows)
    v_prev = (v_out - (1.0 - momentum) * y_out) / momentum

    def input_term(start, count):
        return contract(gate_full, d_gate, 0, 0) + contract(up_full, d_up, 0, 0)

    dx_prev = dx_out + reduce_hidden(input_term, count_rows)
    act_rows, dgate_rows, dup_rows = (
        lax.all_to_all(act, "row", split_axis=0, concat_axis=1, tiled=True),
        lax.all_to_all(d_gate, "row", split_axis=0, concat_axis=1, tiled=True),
        lax.all_to_all(d_up, "row", split_axis=0, concat_axis=1, tiled=True),
    )
    grad_gate = contract(dgate_rows, x_all, 1, 1)
    grad_up = contract(dup_rows, x_all, 1, 1)
    grad_down = contract(act_rows, df_all, 1, 1)
    return (x_prev, v_prev, dx_prev, grad_gate, grad_up, grad_down)


def solution(mesh):
    return jax.shard_map(
        on_device,
        mesh=mesh,
        in_specs=(
            P(("depth", "col"), "row"),
            P(("depth", "col"), "row"),
            P(("depth", "col"), "row"),
            P(("depth", "col"), "row"),
            P(("col", "row"), "depth"),
            P(("col", "row"), "depth"),
            P(("col", "row"), "depth"),
        ),
        out_specs=(
            P(("depth", "col"), "row"),
            P(("depth", "col"), "row"),
            P(("depth", "col"), "row"),
            P(("col", "row"), "depth"),
            P(("col", "row"), "depth"),
            P(("col", "row"), "depth"),
        ),
        check_vma=False,
    )
```

profile of v0, /device:TPU:0, one launch (start us, length us, event | category | flops | bytes accessed | tf_op | source)
XLA Modules:
  0.0 1094.6 jit_solution(1470236012589643987)
XLA Ops:
  7.2 0.0 all-gather.8.cloned.1.call-start
  7.2 2.5 fusion.1
  9.8 0.0 all-gather.12.cloned.1.call-start
  9.8 0.7 all-gather.12.cloned.1.call-update
  10.5 0.0 all-gather.10.cloned.1.call-start
  10.6 0.7 all-gather.10.cloned.1.call-update
  11.3 0.0 all-gather.16.cloned.1.call-start
  11.3 0.3 copy-done.3
  11.7 0.2 copy-done.5
  11.9 0.9 multiply_convert_fusion.3
  12.8 0.0 all-gather.14.cloned.1.call-start
  12.9 0.5 all-gather.14.cloned.1.call-update
  13.4 0.0 all-reduce.3.cloned.1.call-start
  13.4 36.5 %all-gather.8.cloned.1.call-done = bf16[4096,192]{0,1:T(8,128)(2,1)} async-done(((bf16[1024,192]{0,1:T(8,128)(2,1)}), bf16[4096,192]{0,1:T(8,128)(2,1)}) %all-gather.8.cloned.1.call-update) | async-done | bytes 1572880 | tf_op jit(solution)/shard_map/all_gather | solution.py:37
  50.0 178.5 %all-gather.12.cloned.1.call-done = bf16[3584,4096]{1,0:T(8,128)(2,1)} async-done(((bf16[896,4096]{1,0:T(8,128)(2,1)}), bf16[3584,4096]{1,0:T(8,128)(2,1)}) %all-gather.12.cloned.1.call-update) | async-done | bytes 29360144 | tf_op jit(solution)/shard_map/all_gather | solution.py:42
  228.4 18.7 %convolution_bitcast_fusion.1 = f32[3584,192]{0,1:T(8,128)} fusion(bf16[4096,192]{0,1:T(8,128)(2,1)} %all-gather.8.cloned.1.call-done, bf16[3584,4096]{1,0:T(8,128)(2,1)} %all-gather.12.cloned.1.call-done), kind=kOutput, calls=%fused_computation.1 | convolution fusion | flops 5637144576 | bytes 33685504 | tf_op jit(solution)/shard_map/dot_general | solution.py:10
  247.2 160.9 %all-gather.10.cloned.1.call-done = bf16[3584,4096]{1,0:T(8,128)(2,1)} async-done(((bf16[896,4096]{1,0:T(8,128)(2,1)}), bf16[3584,4096]{1,0:T(8,128)(2,1)}) %all-gather.10.cloned.1.call-update) | async-done | bytes 29360144 | tf_op jit(solution)/shard_map/all_gather | solution.py:41
  408.1 16.4 %convolution_bitcast_fusion.2 = f32[3584,192]{0,1:T(8,128)} fusion(bf16[4096,192]{0,1:T(8,128)(2,1)S(1)} %copy-done.4, bf16[3584,4096]{1,0:T(8,128)(2,1)} %all-gather.10.cloned.1.call-done), kind=kOutput, calls=%fused_computation.2 | convolution fusion | flops 5637144576 | bytes 33685504 | tf_op jit(solution)/shard_map/dot_general | solution.py:10
  424.4 22.8 %all-gather.16.cloned.1.call-done = bf16[4096,192]{0,1:T(8,128)(2,1)} async-done(((bf16[1024,192]{0,1:T(8,128)(2,1)}), bf16[4096,192]{0,1:T(8,128)(2,1)}) %all-gather.16.cloned.1.call-update) | async-done | bytes 1572880 | tf_op jit(solution)/shard_map/all_gather | solution.py:38
  447.2 178.3 %all-gather.14.cloned.1.call-done = bf16[3584,4096]{1,0:T(8,128)(2,1)} async-done(((bf16[896,4096]{1,0:T(8,128)(2,1)}), bf16[3584,4096]{1,0:T(8,128)(2,1)}) %all-gather.14.cloned.1.call-update) | async-done | bytes 29360144 | tf_op jit(solution)/shard_map/all_gather | solution.py:43
  625.5 16.2 %convolution_bitcast_fusion = f32[3584,192]{0,1:T(8,128)} fusion(bf16[4096,192]{0,1:T(8,128)(2,1)} %all-gather.16.cloned.1.call-done, bf16[3584,4096]{1,0:T(8,128)(2,1)} %all-gather.14.cloned.1.call-done), kind=kOutput, calls=%fused_computation | convolution fusion | flops 5637144576 | bytes 33685504 | tf_op jit(solution)/shard_map/dot_general | solution.py:10
  641.8 0.0 all-gather.18.cloned.1.call-start
  641.8 0.7 all-gather.18.cloned.1.call-update
  642.6 0.7 all-gather.20.cloned.1.call-update
  643.3 0.0 reduce-scatter.3.cloned.1.call-start
  643.3 194.9 %all-reduce.3.cloned.1.call-done = (f32[3584,192]{0,1:T(8,128)}, f32[3584,192]{0,1:T(8,128)}, f32[3584,192]{0,1:T(8,128)}) async-done(((f32[3584,192]{0,1:T(8,128)}, f32[3584,192]{0,1:T(8,128)}, f32[3584,192]{0,1:T(8,128)}), (f32[3584,192]{0,1:T(8,128)}, f32[3584,192]{0,1:T(8,128)}, f32[3584,192]{0,1:T(8,128)})) %all-reduce.3.cloned.1.call-update) | async-done | bytes 8257552 | tf_op jit(solution)/shard_map/psum | solution.py:50
  838.2 5.0 multiply_convert_fusion
  843.2 16.9 %convolution_bitcast_fusion.3 = f32[4096,192]{0,1:T(8,128)} fusion(bf16[3584,192]{0,1:T(8,128)(2,1)S(1)} %get-tuple-element.13, bf16[3584,4096]{1,0:T(8,128)(2,1)} %all-gather.14.cloned.1.call-done), kind=kOutput, calls=%fused_computation.3 | convolution fusion | flops 5637144576 | bytes 33882112 | tf_op jit(solution)/shard_map/dot_general | solution.py:10
  860.1 0.2 reduce-scatter.5.cloned.1.call-start
  860.3 12.9 %fusion.2 = f32[192,4096]{1,0:T(8,128)S(1)} fusion(bf16[3584,192]{0,1:T(8,128)(2,1)} %get-tuple-element.12, bf16[3584,4096]{1,0:T(8,128)(2,1)} %all-gather.10.cloned.1.call-done), kind=kOutput, calls=%fused_computation.16 | convolution fusion | flops 5637144576 | bytes 33882112 | tf_op jit(solution)/shard_map/dot_general | solution.py:10
  873.2 15.0 %fusion = f32[4096,192]{0,1:T(8,128)} fusion(f32[192,4096]{1,0:T(8,128)S(1)} %fusion.2, bf16[3584,192]{0,1:T(8,128)(2,1)S(1)} %get-tuple-element.11, bf16[3584,4096]{1,0:T(8,128)(2,1)} %all-gather.12.cloned.1.call-done), kind=kOutput, calls=%fused_computation.5 | convolution fusion | flops 5637931008 | bytes 37027840 | tf_op jit(solution)/shard_map/dot_general | solution.py:10
  888.2 1.3 copy-done.1
  889.5 1.2 copy.24
  890.7 3.6 all-to-all-start
  894.3 2.7 copy.23
  897.1 1.2 copy.22
  898.3 28.1 %all-to-all-done = bf16[4,896,192]{1,2,0:T(8,128)(2,1)S(1)} async-done(((bf16[4,896,192]{1,2,0:T(8,128)(2,1)}), bf16[4,896,192]{1,2,0:T(8,128)(2,1)S(1)}, u32[]{:S(2)}, u32[]{:S(2)}) %all-to-all-start) | async-done | bytes 1376288 | tf_op jit(solution)/shard_map/all_to_all | solution.py:66
  926.4 3.5 all-to-all-start.1
  930.0 11.1 %fusion.3 = f32[896,4096]{1,0:T(8,128)} fusion(bf16[896,768]{0,1:T(8,128)(2,1)S(1)} %bitcast.49, bf16[4096,768]{0,1:T(8,128)(2,1)} %all-gather.18.cloned.1.call-done), kind=kOutput, calls=%fused_computation.17 | convolution fusion | flops 5637144576 | bytes 22347776 | tf_op jit(solution)/shard_map/dot_general | solution.py:10
  941.0 19.7 %all-to-all-done.1 = bf16[4,896,192]{1,2,0:T(8,128)(2,1)S(1)} async-done(((bf16[4,896,192]{1,2,0:T(8,128)(2,1)}), bf16[4,896,192]{1,2,0:T(8,128)(2,1)S(1)}, u32[]{:S(2)}, u32[]{:S(2)}) %all-to-all-start.1) | async-done | bytes 1376288 | tf_op jit(solution)/shard_map/all_to_all | solution.py:67
  960.7 3.8 all-to-all-start.2
  964.5 11.1 %fusion.4 = f32[896,4096]{1,0:T(8,128)} fusion(bf16[896,768]{0,1:T(8,128)(2,1)S(1)} %bitcast.50, bf16[4096,768]{0,1:T(8,128)(2,1)} %all-gather.18.cloned.1.call-done), kind=kOutput, calls=%fused_computation.18 | convolution fusion | flops 5637144576 | bytes 22347776 | tf_op jit(solution)/shard_map/dot_general | solution.py:10
  975.6 6.6 all-to-all-done.2
  982.2 11.1 %fusion.5 = f32[896,4096]{1,0:T(8,128)} fusion(bf16[896,768]{0,1:T(8,128)(2,1)S(1)} %bitcast.51, bf16[4096,768]{0,1:T(8,128)(2,1)} %all-gather.20.cloned.1.call-done), kind=kOutput, calls=%fused_computation.19 | convolution fusion | flops 5637144576 | bytes 22347776 | tf_op jit(solution)/shard_map/dot_general | solution.py:10
  993.4 29.8 %reduce-scatter.3.cloned.1.call-done = f32[1024,192]{0,1:T(8,128)} async-done(((f32[4096,192]{0,1:T(8,128)}), f32[1024,192]{0,1:T(8,128)}) %reduce-scatter.3.cloned.1.call-update) | async-done | bytes 786448 | tf_op jit(solution)/shard_map/reduce_scatter | solution.py:16
  1023.2 2.1 subtract_multiply_fusion
  1025.3 60.3 %reduce-scatter.5.cloned.1.call-done = f32[1024,192]{0,1:T(8,128)} async-done(((f32[4096,192]{0,1:T(8,128)}), f32[1024,192]{0,1:T(8,128)}) %reduce-scatter.5.cloned.1.call-update) | async-done | bytes 786448 | tf_op jit(solution)/shard_map/reduce_scatter | solution.py:16
  1085.7 2.1 add.33
  (17 shorter events, 0.2 us)
Async XLA Ops:
  7.2 42.8 %all-gather.8.cloned.1.call-start = ((), (), s32[]{:S(2)}) async-start(), calls=%async_computation.5 | async-start | bytes 1966080 | tf_op jit(solution)/shard_map/all_gather | solution.py:37
  9.8 218.7 %all-gather.12.cloned.1.call-start = ((), (), s32[]{:S(2)}) async-start(), calls=%async_computation.7 | async-start | bytes 36700160 | tf_op jit(solution)/shard_map/all_gather | solution.py:42
  10.5 1.1 copy-start.3
  10.5 1.4 copy-start.5
  10.5 397.5 %all-gather.10.cloned.1.call-start = ((), (), s32[]{:S(2)}) async-start(), calls=%async_computation.6 | async-start | bytes 36700160 | tf_op jit(solution)/shard_map/all_gather | solution.py:41
  11.3 435.9 %all-gather.16.cloned.1.call-start = ((), (), s32[]{:S(2)}) async-start(), calls=%async_computation.10 | async-start | bytes 1966080 | tf_op jit(solution)/shard_map/all_gather | solution.py:38
  12.8 612.7 %all-gather.14.cloned.1.call-start = ((), (), s32[]{:S(2)}) async-start(), calls=%async_computation.8 | async-start | bytes 36700160 | tf_op jit(solution)/shard_map/all_gather | solution.py:43
  13.4 824.8 %all-reduce.3.cloned.1.call-start = ((), (), s32[]{:S(2)}) async-start(), calls=%async_computation.14 | async-start | bytes 16515072 | tf_op jit(solution)/shard_map/psum | solution.py:50
  50.0 358.1 %copy-start.4 = (bf16[4096,192]{0,1:T(8,128)(2,1)S(1)}, bf16[4096,192]{0,1:T(8,128)(2,1)}, u32[]{:S(2)}) copy-start(bf16[4096,192]{0,1:T(8,128)(2,1)} %all-gather.8.cloned.1.call-done) | copy-start | bytes 4718596
  641.8 288.2 %all-gather.18.cloned.1.call-start = ((), (), s32[]{:S(2)}) async-start(), calls=%async_computation.12 | async-start | bytes 7864320 | tf_op jit(solution)/shard_map/all_gather | solution.py:44
  642.5 333.1 %all-gather.20.cloned.1.call-start = ((), (), s32[]{:S(2)}) async-start(), calls=%async_computation.13 | async-start | bytes 7864320 | tf_op jit(solution)/shard_map/all_gather | solution.py:45
  643.3 379.9 %reduce-scatter.3.cloned.1.call-start = ((), (), s32[]{:S(2)}) async-start(), calls=%async_computation.9 | async-start | bytes 3932160 | tf_op jit(solution)/shard_map/reduce_scatter | solution.py:16
  843.2 30.0 %copy-start = (bf16[3584,192]{0,1:T(8,128)(2,1)}, bf16[3584,192]{0,1:T(8,128)(2,1)S(1)}, u32[]{:S(2)}) copy-start(bf16[3584,192]{0,1:T(8,128)(2,1)S(1)} %get-tuple-element.11) | copy-start | bytes 4128772
  860.1 225.6 %reduce-scatter.5.cloned.1.call-start = ((), (), s32[]{:S(2)}) async-start(), calls=%async_computation.11 | async-start | bytes 3932160 | tf_op jit(solution)/shard_map/reduce_scatter | solution.py:16
  888.2 1.3 copy-start.1
  890.7 35.6 %all-to-all-start = ((bf16[4,896,192]{1,2,0:T(8,128)(2,1)}), bf16[4,896,192]{1,2,0:T(8,128)(2,1)S(1)}, u32[]{:S(2)}, u32[]{:S(2)}) async-start(bf16[4,896,192]{1,2,0:T(8,128)(2,1)} %bitcast.57), calls=%async_computation.2 | async-start | bytes 2752512 | tf_op jit(solution)/shard_map/all_to_all | solution.py:66
  926.4 34.4 %all-to-all-start.1 = ((bf16[4,896,192]{1,2,0:T(8,128)(2,1)}), bf16[4,896,192]{1,2,0:T(8,128)(2,1)S(1)}, u32[]{:S(2)}, u32[]{:S(2)}) async-start(bf16[4,896,192]{1,2,0:T(8,128)(2,1)} %bitcast.56), calls=%async_computation.3 | async-start | bytes 2752512 | tf_op jit(solution)/shard_map/all_to_all | solution.py:67
  960.7 21.5 %all-to-all-start.2 = ((bf16[4,896,192]{1,2,0:T(8,128)(2,1)}), bf16[4,896,192]{1,2,0:T(8,128)(2,1)S(1)}, u32[]{:S(2)}, u32[]{:S(2)}) async-start(bf16[4,896,192]{1,2,0:T(8,128)(2,1)} %bitcast.55), calls=%async_computation.4 | async-start | bytes 2752512 | tf_op jit(solution)/shard_map/all_to_all | solution.py:65
  982.2 41.0 %copy-start.2 = (f32[1024,192]{0,1:T(8,128)S(1)}, f32[1024,192]{0,1:T(8,128)}, u32[]{:S(2)}) copy-start(f32[1024,192]{0,1:T(8,128)} %param.8) | copy-start | bytes 2359300
Sparse Core Ops, SparseCore 0:
  10.1 39.7 all-gather.7
  51.5 176.8 all-gather.11
  230.0 178.0 all-gather.9
  410.1 37.0 all-gather.15
  448.6 176.8 all-gather.13
  641.9 196.2 all-reduce.2
  839.7 46.3 all-gather.17
  887.7 72.6 all-gather.19
  962.7 60.4 reduce-scatter.2
  1025.3 60.2 reduce-scatter.4
where the time goes:
time: 1100 us; the launch traced here: 1090 us
  waiting for transfers between devices  920 us (84%)
  matrix products  129 us (12%)
  between operations  14.2 us (1%)
  other arithmetic  12.7 us (1%)
  starting transfers between devices  11.5 us (1%)
    psum x1, waiting for transfers between devices, on_device(): gate, up_val, d_act = lax.psum((gate_part, up_part, dact_part), 'depth')  195 us
    all_gather x1, waiting for transfers between devices, on_device(): lax.all_gather(up_weight, 'row', axis=0, tiled=True)  178 us
    all_gather x1, waiting for transfers between devices, on_device(): lax.all_gather(down_weight, 'row', axis=0, tiled=True)  178 us
    all_gather x1, waiting for transfers between devices, on_device(): lax.all_gather(gate_weight, 'row', axis=0, tiled=True)  161 us
    dot_general x9, matrix products, contract(): lax.dot_general(left, right, (((left_dim,), (right_dim,)), ((), ())), pre...  129 us
    reduce_scatter x2, waiting for transfers between devices, reduce_hidden(): lax.psum_scatter(term_fn(jnp.int32(0), count_rows * lax.axis_size('col'))...  90.2 us
    all_gather x1, waiting for transfers between devices, on_device(): lax.all_gather(x_half, 'col', axis=0, tiled=True)  36.5 us
    all_to_all x1, waiting for transfers between devices, on_device(): lax.all_to_all(d_gate, 'row', split_axis=0, concat_axis=1, tiled=True)  28.1 us
  transfers between devices with their start and end apart: 13, of which 11 were waited for; matrix products, arithmetic and copies ran while one was open for 12% of the time, Pallas kernels for 0%

commit v1 on v0

v1 whole, which is shorter than its diff:
```python
import jax
import jax.numpy as jnp
from jax import lax
from jax.sharding import PartitionSpec as P

momentum = 0.5
CHUNKS = 3
BF = jnp.bfloat16
F32 = jnp.float32


def contract(left, right, left_dim, right_dim):
    return lax.dot_general(
        left, right, (((left_dim,), (right_dim,)), ((), ())), preferred_element_type=F32
    )


def swap(value, axis, mask):
    n = lax.axis_size(axis)
    return lax.ppermute(value, axis, [(i, i ^ mask) for i in range(n)])


def row_masks():
    masks, m = [], lax.axis_size("row") // 2
    while m:
        masks.append(m)
        m //= 2
    return masks


def gather_tokens(block):
    cols = lax.all_gather(block, "col", axis=0, tiled=False)
    n, t, f = cols.shape
    out = cols.transpose(1, 0, 2).reshape(t, n * f)
    for mask in row_masks():
        out = jnp.concatenate([out, swap(out, "row", mask)], axis=0)
    return out


def depth_sum(part):
    if lax.axis_size("depth") == 2:
        return part + swap(part.astype(BF), "depth", 1).astype(F32)
    return lax.psum(part, "depth")


def scatter_tokens(term):
    masks = row_masks()[::-1]
    total_rows = term.rows
    half = total_rows // 2
    got = swap(term(half, total_rows).astype(BF), "row", masks[0])
    kept = term(0, half) + got.astype(F32)
    for mask in masks[1:]:
        half //= 2
        got = swap(kept[half:].astype(BF), "row", mask)
        kept = kept[:half] + got.astype(F32)
    n = lax.axis_size("col")
    t, f = kept.shape
    blocks = kept.astype(BF).reshape(t, n, f // n).transpose(1, 0, 2)
    return lax.psum_scatter(blocks, "col", scatter_dimension=0, tiled=False)


class Term:
    def __init__(self, rows, fn):
        self.rows, self.fn = rows, fn

    def __call__(self, lo, hi):
        return self.fn(lo, hi)


def nonlinear(gate, up_val, d_act):
    sig = jax.nn.sigmoid(gate)
    act = (gate * sig * up_val).astype(BF)
    d_gate = (d_act * up_val * sig * (1.0 + gate * (1.0 - sig))).astype(BF)
    d_up = (d_act * gate * sig).astype(BF)
    return (act, d_gate, d_up)


def on_device(x_out, v_out, dx_out, dv_out, gate_weight, up_weight, down_weight):
    x_prev = x_out - v_out
    x_tok = x_prev.astype(BF).T
    df_tok = ((1.0 - momentum) * (dx_out + dv_out)).astype(BF).T
    tokens = x_tok.shape[0]
    t = tokens // CHUNKS
    xs, dfs, acts, dgates, dups, ys, dxs = [], [], [], [], [], [], []
    for c in range(CHUNKS):
        xs.append(gather_tokens(x_tok[c * t : (c + 1) * t]))
        dfs.append(gather_tokens(df_tok[c * t : (c + 1) * t]))
    for c in range(CHUNKS):
        gate = depth_sum(contract(xs[c], gate_weight, 1, 1))
        up_val = depth_sum(contract(xs[c], up_weight, 1, 1))
        d_act = depth_sum(contract(dfs[c], down_weight, 1, 1))
        act, d_gate, d_up = nonlinear(gate, up_val, d_act)
        acts.append(act)
        dgates.append(d_gate)
        dups.append(d_up)
        rows = act.shape[0]

        def down_term(lo, hi, act=act):
            return contract(act[lo:hi], down_weight, 1, 0)

        def input_term(lo, hi, d_gate=d_gate, d_up=d_up):
            return contract(d_gate[lo:hi], gate_weight, 1, 0) + contract(
                d_up[lo:hi], up_weight, 1, 0
            )

        ys.append(scatter_tokens(Term(rows, down_term)))
        dxs.append(scatter_tokens(Term(rows, input_term)))
    x_all, df_all = jnp.concatenate(xs, 0), jnp.concatenate(dfs, 0)
    grad_gate = contract(jnp.concatenate(dgates, 0), x_all, 0, 0)
    grad_up = contract(jnp.concatenate(dups, 0), x_all, 0, 0)
    grad_down = contract(jnp.concatenate(acts, 0), df_all, 0, 0)
    y_out = jnp.concatenate(ys, 0).astype(F32).T
    dx_sum = jnp.concatenate(dxs, 0).astype(F32).T
    v_prev = (v_out - (1.0 - momentum) * y_out) / momentum
    dx_prev = dx_out + dx_sum
    return (x_prev, v_prev, dx_prev, grad_gate, grad_up, grad_down)


def solution(mesh):
    act_spec, weight_spec = P(("depth", "col"), "row"), P(("col", "row"), "depth")
    return jax.shard_map(
        on_device,
        mesh=mesh,
        in_specs=(act_spec,) * 4 + (weight_spec,) * 3,
        out_specs=(act_spec,) * 3 + (weight_spec,) * 3,
        check_vma=False,
    )
```

time: 1100 us -> 454 us (0.41)
  waiting for transfers between devices: 920 us -> 128 us
  blocking collectives: 0 us -> 97 us
  local copies, waits for them, and re-layouts: 7.03 us -> 39.8 us
  starting transfers between devices: 11.5 us -> 23.7 us
    all_gather x7 -> x0, waiting for transfers between devices: 577 us -> none  [the longest x1 178 us: on_device(): lax.all_gather(up_weight, 'row', axis=0, tiled=True)]
    psum x1 -> x0, waiting for transfers between devices: 195 us -> none  [on_device(): gate, up_val, d_act = lax.psum((gate_part, up_part, dact_part), 'depth')]
    all_gather x0 -> x6, blocking collectives: none -> 97 us  [gather_tokens(): cols = lax.all_gather(block, 'col', axis=0, tiled=False)]
    ppermute x0 -> x33, waiting for transfers between devices: none -> 71.7 us  [swap(): return lax.ppermute(value, axis, [(i, i ^ mask) for i in range(n)])]
    all_to_all x3 -> x0, waiting for transfers between devices: 54.4 us -> none  [the longest x1 28.1 us: on_device(): lax.all_to_all(d_gate, 'row', split_axis=0, concat_axis=1, tiled=True)]
    reduce_scatter x2 -> x6, waiting for transfers between devices: 90.2 us -> 55.9 us  [scatter_tokens(): return lax.psum_scatter(blocks, 'col', scatter_dimension=0, tiled=False)]
    unnamed x12 -> x122, local copies, waits for them, and re-layouts: 1.9 us -> 25.2 us
    ppermute x0 -> x33, starting transfers between devices: none -> 23.2 us  [swap(): return lax.ppermute(value, axis, [(i, i ^ mask) for i in range(n)])]
  transfers between devices with their start and end apart: 13 -> 39, of which waited for: 11 -> 13; matrix products, arithmetic and copies ran while one was open for 12% -> 38% of each run, Pallas kernels for 0% -> 0%
where the time goes in v1:
time: 454 us; the launch traced here: 449 us
  waiting for transfers between devices  128 us (28%)
  matrix products  124 us (27%)
  blocking collectives  97 us (21%)
  local copies, waits for them, and re-layouts  39.8 us (9%)
  starting transfers between devices  23.7 us (5%)
  other arithmetic  21.9 us (5%)
  between operations  15.3 us (3%)
    dot_general x30, matrix products, contract(): lax.dot_general(left, right, (((left_dim,), (right_dim,)), ((), ())), pre...  124 us
    all_gather x6, blocking collectives, gather_tokens(): cols = lax.all_gather(block, 'col', axis=0, tiled=False)  97 us
    ppermute x33, waiting for transfers between devices, swap(): return lax.ppermute(value, axis, [(i, i ^ mask) for i in range(n)])  71.7 us
    reduce_scatter x6, waiting for transfers between devices, scatter_tokens(): return lax.psum_scatter(blocks, 'col', scatter_dimension=0, tiled=False)  55.9 us
    unnamed x122, local copies, waits for them, and re-layouts  25.2 us
    ppermute x33, starting transfers between devices, swap(): return lax.ppermute(value, axis, [(i, i ^ mask) for i in range(n)])  23.2 us
  transfers between devices with their start and end apart: 39, of which 13 were waited for; matrix products, arithmetic and copies ran while one was open for 38% of the time, Pallas kernels for 0%

profile of v1, /device:TPU:0, one launch (start us, length us, event | category | flops | bytes accessed | tf_op | source)
XLA Modules:
  0.0 449.2 jit_solution(12414105475170221567)
XLA Ops:
  8.8 17.5 %all-gather.4 = bf16[256,1024]{1,0:T(8,128)(2,1)S(1)} all-gather(bf16[64,1024]{1,0:T(8,128)(2,1)S(1)} %get-tuple-element.37), channel_id=6, replica_groups=mesh['depth'=2,'row'=4,'col'=4] {'col'}, dimensions={0}, use_global_device_ids=true | all-gather | bytes 655360 | tf_op jit(solution)/shard_map/all_gather | solution.py:32
  28.4 16.2 %all-gather.5 = bf16[256,1024]{1,0:T(8,128)(2,1)S(1)} all-gather(bf16[64,1024]{1,0:T(8,128)(2,1)S(1)} %get-tuple-element.36), channel_id=7, replica_groups=mesh['depth'=2,'row'=4,'col'=4] {'col'}, dimensions={0}, use_global_device_ids=true | all-gather | bytes 655360 | tf_op jit(solution)/shard_map/all_gather | solution.py:32
  45.7 16.1 %all-gather.3 = bf16[256,1024]{1,0:T(8,128)(2,1)S(1)} all-gather(bf16[64,1024]{1,0:T(8,128)(2,1)S(1)} %get-tuple-element.35), channel_id=5, replica_groups=mesh['depth'=2,'row'=4,'col'=4] {'col'}, dimensions={0}, use_global_device_ids=true | all-gather | bytes 655360 | tf_op jit(solution)/shard_map/all_gather | solution.py:32
  64.5 16.4 %all-gather.1 = bf16[256,1024]{1,0:T(8,128)(2,1)S(1)} all-gather(bf16[64,1024]{1,0:T(8,128)(2,1)S(1)} %get-tuple-element.40), channel_id=3, replica_groups=mesh['depth'=2,'row'=4,'col'=4] {'col'}, dimensions={0}, use_global_device_ids=true | all-gather | bytes 655360 | tf_op jit(solution)/shard_map/all_gather | solution.py:32
  81.7 15.9 %all-gather = bf16[256,1024]{1,0:T(8,128)(2,1)S(1)} all-gather(bf16[64,1024]{1,0:T(8,128)(2,1)S(1)} %get-tuple-element.38), channel_id=2, replica_groups=mesh['depth'=2,'row'=4,'col'=4] {'col'}, dimensions={0}, use_global_device_ids=true | all-gather | bytes 655360 | tf_op jit(solution)/shard_map/all_gather | solution.py:32
  98.2 2.4 collective-permute-start
  102.3 14.9 %all-gather.2 = bf16[256,1024]{1,0:T(8,128)(2,1)S(1)} all-gather(bf16[64,1024]{1,0:T(8,128)(2,1)S(1)} %get-tuple-element.39), channel_id=4, replica_groups=mesh['depth'=2,'row'=4,'col'=4] {'col'}, dimensions={0}, use_global_device_ids=true | all-gather | bytes 655360 | tf_op jit(solution)/shard_map/all_gather | solution.py:32
  120.9 6.1 %collective-permute-done.12 = bf16[64,4096]{1,0:T(8,128)(2,1)S(1)} collective-permute-done((bf16[64,4096]{1,0:T(8,128)(2,1)S(1)}, bf16[64,4096]{1,0:T(8,128)(2,1)S(1)}, u32[]{:S(2)}, u32[]{:S(2)}) %collective-permute-start.12) | collective-permute-done | bytes 524320 | tf_op jit(solution)/shard_map/ppermute | solution.py:20
  131.6 3.5 fusion.100
  136.7 3.4 fusion.94
  144.3 5.6 %fusion.102 = (bf16[256,896]{1,0:T(8,128)(2,1)}, f32[256,896]{1,0:T(8,128)}) fusion(bf16[256,4096]{1,0:T(8,128)(2,1)} %copy-done.37, bf16[896,4096]{1,0:T(8,128)(2,1)S(1)} %bitcast.123), kind=kOutput, calls=%fused_computation.181 | convolution fusion | flops 1879277568 | bytes 10813440 | tf_op jit(solution)/shard_map/dot_general | solution.py:13
  151.0 3.7 fusion.101
  154.7 2.8 constant_dynamic-update-slice_fusion.12
  157.5 5.6 %fusion.99 = (bf16[256,896]{1,0:T(8,128)(2,1)}, f32[256,896]{1,0:T(8,128)}) fusion(bf16[256,4096]{1,0:T(8,128)(2,1)} %get-tuple-element.20, bf16[896,4096]{1,0:T(8,128)(2,1)S(1)} %bitcast.123), kind=kOutput, calls=%fused_computation.178 | convolution fusion | flops 1879277568 | bytes 10813440 | tf_op jit(solution)/shard_map/dot_general | solution.py:13
  165.2 3.7 fusion.98
  170.5 5.0 %fusion.96 = (bf16[256,896]{1,0:T(8,128)(2,1)}, f32[256,896]{1,0:T(8,128)}) fusion(bf16[256,4096]{1,0:T(8,128)(2,1)} %get-tuple-element.18, bf16[896,4096]{1,0:T(8,128)(2,1)S(1)} %bitcast.123), kind=kOutput, calls=%fused_computation.175 | convolution fusion | flops 1879277568 | bytes 10813440 | tf_op jit(solution)/shard_map/dot_general | solution.py:13
  175.5 4.9 %fusion.95 = (bf16[256,896]{1,0:T(8,128)(2,1)S(1)}, f32[256,896]{1,0:T(8,128)}) fusion(bf16[256,4096]{1,0:T(8,128)(2,1)} %get-tuple-element.18, bf16[896,4096]{1,0:T(8,128)(2,1)S(1)} %bitcast.119), kind=kOutput, calls=%fused_computation.174 | convolution fusion | flops 1879277568 | bytes 10813440 | tf_op jit(solution)/shard_map/dot_general | solution.py:13
  180.4 4.8 %fusion.97 = (bf16[256,896]{1,0:T(8,128)(2,1)}, f32[256,896]{1,0:T(8,128)}) fusion(bf16[896,4096]{1,0:T(8,128)(2,1)S(1)} %bitcast.121, bf16[128,4096]{1,0:T(8,128)(2,1)} %collective-permute-done.24, bf16[64,4096]{1,0:T(8,128)(2,1)S(1)} %collective-permute-done.23, bf16[64,4096]{1,0:T(8,128)(2,1)S(1)} %bitcast.135), kind=kOutput, calls=%fused_computation.176 | convolution fusion | flops 1885569024 | bytes 10813440 | tf_op jit(solution)/shard_map/dot_general | solution.py:13
  189.4 2.3 constant_dynamic-update-slice_fusion.21
  197.0 11.5 %collective-permute-done.15 = bf16[256,896]{1,0:T(8,128)(2,1)S(1)} collective-permute-done((bf16[256,896]{1,0:T(8,128)(2,1)S(1)}, bf16[256,896]{1,0:T(8,128)(2,1)S(1)}, u32[]{:S(2)}, u32[]{:S(2)}) %collective-permute-start.15) | collective-permute-done | bytes 458784 | tf_op jit(solution)/shard_map/ppermute | solution.py:20
  210.1 8.3 %collective-permute-done.14 = bf16[256,896]{1,0:T(8,128)(2,1)S(1)} collective-permute-done((bf16[256,896]{1,0:T(8,128)(2,1)S(1)}, bf16[256,896]{1,0:T(8,128)(2,1)S(1)}, u32[]{:S(2)}, u32[]{:S(2)}) %collective-permute-start.14) | collective-permute-done | bytes 458784 | tf_op jit(solution)/shard_map/ppermute | solution.py:20
  219.9 2.5 multiply_convert_fusion
  223.9 2.7 fusion.53
  227.1 11.0 %collective-permute-done.9 = bf16[256,896]{1,0:T(8,128)(2,1)S(1)} collective-permute-done((bf16[256,896]{1,0:T(8,128)(2,1)S(1)}, bf16[256,896]{1,0:T(8,128)(2,1)S(1)}, u32[]{:S(2)}, u32[]{:S(2)}) %collective-permute-start.9) | collective-permute-done | bytes 458784 | tf_op jit(solution)/shard_map/ppermute | solution.py:20
  238.1 9.8 %collective-permute-done.8 = bf16[256,896]{1,0:T(8,128)(2,1)S(1)} collective-permute-done((bf16[256,896]{1,0:T(8,128)(2,1)}, bf16[256,896]{1,0:T(8,128)(2,1)S(1)}, u32[]{:S(2)}, u32[]{:S(2)}) %collective-permute-start.8) | collective-permute-done | bytes 458784 | tf_op jit(solution)/shard_map/ppermute | solution.py:20
  251.2 5.4 %collective-permute-done.2 = bf16[256,896]{1,0:T(8,128)(2,1)S(1)} collective-permute-done((bf16[256,896]{1,0:T(8,128)(2,1)S(1)}, bf16[256,896]{1,0:T(8,128)(2,1)S(1)}, u32[]{:S(2)}, u32[]{:S(2)}) %collective-permute-start.2) | collective-permute-done | bytes 458784 | tf_op jit(solution)/shard_map/ppermute | solution.py:20
  258.4 2.3 convolution_convert_fusion.2
  260.7 2.4 convolution_convert_fusion.1
  263.6 2.3 convolution_convert_fusion
  265.9 2.3 fusion.1
  272.5 11.1 %fusion.27 = f32[896,4096]{1,0:T(8,128)} fusion(bf16[768,4096]{1,0:T(8,128)(2,1)} %get-tuple-element.17, bf16[256,896]{1,0:T(8,128)(2,1)S(1)} %copy-done.16, bf16[256,896]{1,0:T(8,128)(2,1)S(1)} %get-tuple-element.11, bf16[256,896]{1,0:T(8,128)(2,1)S(1)} %get-tuple-element.8), kind=kOutput, calls=%fused_computation.42 | convolution fusion | flops 5641273344 | bytes 22347776 | tf_op jit(solution)/shard_map/dot_general | solution.py:13
  283.6 2.3 fusion.2
  286.0 2.6 fusion.69
  289.1 2.5 convert_add_fusion.5
  291.7 2.6 convert_add_fusion.4
  296.5 9.0 %collective-permute-done.5 = bf16[64,4096]{1,0:T(8,128)(2,1)S(1)} collective-permute-done((bf16[64,4096]{1,0:T(8,128)(2,1)S(1)}, bf16[64,4096]{1,0:T(8,128)(2,1)S(1)}, u32[]{:S(2)}, u32[]{:S(2)}) %collective-permute-start.5) | collective-permute-done | bytes 524320 | tf_op jit(solution)/shard_map/ppermute | solution.py:20
  306.9 4.8 %convert_add_fusion.3 = f32[128,4096]{1,0:T(8,128)S(1)} fusion(bf16[128,4096]{1,0:T(8,128)(2,1)} %collective-permute-done.16, bf16[896,4096]{1,0:T(8,128)(2,1)} %param.13, bf16[256,896]{1,0:T(8,128)(2,1)} %copy-done.11), kind=kOutput, calls=%fused_computation.33 | convolution fusion | flops 940572672 | bytes 10715136 | tf_op jit(solution)/shard_map/dot_general | solution.py:13
  315.6 5.1 %collective-permute-done.11 = bf16[64,4096]{1,0:T(8,128)(2,1)} collective-permute-done((bf16[64,4096]{1,0:T(8,128)(2,1)}, bf16[64,4096]{1,0:T(8,128)(2,1)}, u32[]{:S(2)}, u32[]{:S(2)}) %collective-permute-start.11) | collective-permute-done | bytes 524320 | tf_op jit(solution)/shard_map/ppermute | solution.py:20
  323.1 5.5 %convert_add_fusion = f32[128,4096]{1,0:T(8,128)S(1)} fusion(bf16[128,4096]{1,0:T(8,128)(2,1)} %collective-permute-done.31, f32[128,4096]{1,0:T(8,128)} %fusion.53, bf16[896,4096]{1,0:T(8,128)(2,1)} %param.12, bf16[256,896]{1,0:T(8,128)(2,1)} %get-tuple-element.14), kind=kOutput, calls=%fused_computation.30 | convolution fusion | flops 941096960 | bytes 12812288 | tf_op jit(solution)/shard_map/dot_general | solution.py:13
  333.2 4.9 %convert_add_fusion.1 = f32[128,4096]{1,0:T(8,128)S(1)} fusion(bf16[128,4096]{1,0:T(8,128)(2,1)} %collective-permute-done.26, f32[128,4096]{1,0:T(8,128)S(1)} %fusion.61, bf16[896,4096]{1,0:T(8,128)(2,1)} %param.12, bf16[256,896]{1,0:T(8,128)(2,1)} %copy-done.15), kind=kOutput, calls=%fused_computation.31 | convolution fusion | flops 941096960 | bytes 12812288 | tf_op jit(solution)/shard_map/dot_general | solution.py:13
  340.8 2.8 collective-permute-done.32
  345.8 4.8 %convert_add_fusion.2 = f32[128,4096]{1,0:T(8,128)S(1)} fusion(bf16[128,4096]{1,0:T(8,128)(2,1)} %collective-permute-done.21, f32[128,4096]{1,0:T(8,128)S(1)} %copy-done, bf16[896,4096]{1,0:T(8,128)(2,1)} %param.12, bf16[256,896]{1,0:T(8,128)(2,1)} %copy-done.14), kind=kOutput, calls=%fused_computation.32 | convolution fusion | flops 941096960 | bytes 12812288 | tf_op jit(solution)/shard_map/dot_general | solution.py:13
  352.5 2.4 collective-permute-done.27
  357.0 11.3 %fusion.21 = f32[896,4096]{1,0:T(8,128)} fusion(bf16[768,4096]{1,0:T(8,128)(2,1)} %get-tuple-element.17, bf16[256,896]{1,0:T(8,128)(2,1)S(1)} %get-tuple-element.15, bf16[256,896]{1,0:T(8,128)(2,1)S(1)} %get-tuple-element.12, bf16[256,896]{1,0:T(8,128)(2,1)S(1)} %get-tuple-element.9), kind=kOutput, calls=%fused_computation.36 | convolution fusion | flops 5641273344 | bytes 22347776 | tf_op jit(solution)/shard_map/dot_general | solution.py:13
  370.3 11.6 %fusion.33 = f32[896,4096]{1,0:T(8,128)} fusion(bf16[768,4096]{1,0:T(8,128)(2,1)} %constant_dynamic-update-slice_fusion.18, bf16[256,896]{1,0:T(8,128)(2,1)} %copy-done.11, bf16[256,896]{1,0:T(8,128)(2,1)} %copy-done.12, bf16[256,896]{1,0:T(8,128)(2,1)} %copy-done.13), kind=kOutput, calls=%fused_computation.48 | convolution fusion | flops 5641273344 | bytes 22347776 | tf_op jit(solution)/shard_map/dot_general | solution.py:13
  384.0 12.1 %reduce-scatter.17.cloned.1.call-done = bf16[1,64,1024]{2,1,0:T(8,128)(2,1)} async-done(((bf16[4,64,1024]{2,1,0:T(8,128)(2,1)}), bf16[1,64,1024]{2,1,0:T(8,128)(2,1)}) %reduce-scatter.17.cloned.1.call-update) | async-done | bytes 131088 | tf_op jit(solution)/shard_map/reduce_scatter | solution.py:59
  396.0 21.9 %reduce-scatter.15.cloned.1.call-done = bf16[1,64,1024]{2,1,0:T(8,128)(2,1)} async-done(((bf16[4,64,1024]{2,1,0:T(8,128)(2,1)}), bf16[1,64,1024]{2,1,0:T(8,128)(2,1)}) %reduce-scatter.15.cloned.1.call-update) | async-done | bytes 131088 | tf_op jit(solution)/shard_map/reduce_scatter | solution.py:59
  418.0 21.9 %reduce-scatter.13.cloned.1.call-done = bf16[1,64,1024]{2,1,0:T(8,128)(2,1)} async-done(((bf16[4,64,1024]{2,1,0:T(8,128)(2,1)}), bf16[1,64,1024]{2,1,0:T(8,128)(2,1)}) %reduce-scatter.13.cloned.1.call-update) | async-done | bytes 131088 | tf_op jit(solution)/shard_map/reduce_scatter | solution.py:59
  (238 shorter events, 83.4 us)
Async XLA Ops:
  7.2 374.8 %reduce-scatter.7.cloned.1.call-start = ((), (), s32[]{:S(2)}) async-start(), calls=%async_computation.6 | async-start | bytes 655360 | tf_op jit(solution)/shard_map/reduce_scatter | solution.py:59
  8.8 54.7 %copy-start.17 = (f32[1024,192]{0,1:T(8,128)S(1)}, f32[1024,192]{0,1:T(8,128)}, u32[]{:S(2)}) copy-start(f32[1024,192]{0,1:T(8,128)} %param.8) | copy-start | bytes 2359300
  8.8 54.7 %copy-start.33 = (f32[1024,192]{0,1:T(8,128)S(1)}, f32[1024,192]{0,1:T(8,128)}, u32[]{:S(2)}) copy-start(f32[1024,192]{0,1:T(8,128)} %param.7) | copy-start | bytes 2359300
  26.9 90.9 %collective-permute-start.23 = (bf16[64,4096]{1,0:T(8,128)(2,1)S(1)}, bf16[64,4096]{1,0:T(8,128)(2,1)S(1)}, u32[]{:S(2)}, u32[]{:S(2)}) collective-permute-start(bf16[64,4096]{1,0:T(8,128)(2,1)S(1)} %bitcast.133), channel_id=1, source_target_pairs={{0,8},{4,12},{8,0},{12,4},{1,9},{5,13},{9,1},{13,5},{2,10},{6,14},... | collective-permute-start | bytes 1572872 | tf_op jit(solution)/shard_map/ppermute | solution.py:20
  45.2 73.8 %collective-permute-start.28 = (bf16[64,4096]{1,0:T(8,128)(2,1)S(1)}, bf16[64,4096]{1,0:T(8,128)(2,1)S(1)}, u32[]{:S(2)}, u32[]{:S(2)}) collective-permute-start(bf16[64,4096]{1,0:T(8,128)(2,1)S(1)} %bitcast.137), channel_id=1, source_target_pairs={{0,8},{4,12},{8,0},{12,4},{1,9},{5,13},{9,1},{13,5},{2,10},{6,14},... | collective-permute-start | bytes 1572872 | tf_op jit(solution)/shard_map/ppermute | solution.py:20
  62.5 56.6 %collective-permute-start.18 = (bf16[64,4096]{1,0:T(8,128)(2,1)S(1)}, bf16[64,4096]{1,0:T(8,128)(2,1)S(1)}, u32[]{:S(2)}, u32[]{:S(2)}) collective-permute-start(bf16[64,4096]{1,0:T(8,128)(2,1)S(1)} %bitcast.141), channel_id=1, source_target_pairs={{0,8},{4,12},{8,0},{12,4},{1,9},{5,13},{9,1},{13,5},{2,10},{6,14},... | collective-permute-start | bytes 1572872 | tf_op jit(solution)/shard_map/ppermute | solution.py:20
  81.5 38.2 %collective-permute-start.6 = (bf16[64,4096]{1,0:T(8,128)(2,1)S(1)}, bf16[64,4096]{1,0:T(8,128)(2,1)S(1)}, u32[]{:S(2)}, u32[]{:S(2)}) collective-permute-start(bf16[64,4096]{1,0:T(8,128)(2,1)S(1)} %bitcast.127), channel_id=1, source_target_pairs={{0,8},{4,12},{8,0},{12,4},{1,9},{5,13},{9,1},{13,5},{2,10},{6,14},... | collective-permute-start | bytes 1572872 | tf_op jit(solution)/shard_map/ppermute | solution.py:20
  98.2 29.9 %collective-permute-start = (bf16[64,4096]{1,0:T(8,128)(2,1)S(1)}, bf16[64,4096]{1,0:T(8,128)(2,1)S(1)}, u32[]{:S(2)}, u32[]{:S(2)}) collective-permute-start(bf16[64,4096]{1,0:T(8,128)(2,1)S(1)} %bitcast.130), channel_id=1, source_target_pairs={{0,8},{4,12},{8,0},{12,4},{1,9},{5,13},{9,1},{13,5},{2,10},{6,14},... | collective-permute-start | bytes 1572872 | tf_op jit(solution)/shard_map/ppermute | solution.py:20
  117.8 9.2 %collective-permute-start.12 = (bf16[64,4096]{1,0:T(8,128)(2,1)S(1)}, bf16[64,4096]{1,0:T(8,128)(2,1)S(1)}, u32[]{:S(2)}, u32[]{:S(2)}) collective-permute-start(bf16[64,4096]{1,0:T(8,128)(2,1)S(1)} %bitcast.124), channel_id=1, source_target_pairs={{0,8},{4,12},{8,0},{12,4},{1,9},{5,13},{9,1},{13,5},{2,10},{6,14},... | collective-permute-start | bytes 1572872 | tf_op jit(solution)/shard_map/ppermute | solution.py:20
  118.9 61.4 %collective-permute-start.24 = (bf16[128,4096]{1,0:T(8,128)(2,1)}, bf16[128,4096]{1,0:T(8,128)(2,1)}, u32[]{:S(2)}, u32[]{:S(2)}) collective-permute-start(bf16[128,4096]{1,0:T(8,128)(2,1)} %pad_maximum_fusion.4), channel_id=1, source_target_pairs={{0,4},{4,0},{8,12},{12,8},{1,5},{5,1},{9,13},{13,9},{2,6},{6,2},{1... | collective-permute-start | bytes 3145736 | tf_op jit(solution)/shard_map/ppermute | solution.py:20
  119.0 16.0 %collective-permute-start.29 = (bf16[128,4096]{1,0:T(8,128)(2,1)S(1)}, bf16[128,4096]{1,0:T(8,128)(2,1)S(1)}, u32[]{:S(2)}, u32[]{:S(2)}) collective-permute-start(bf16[128,4096]{1,0:T(8,128)(2,1)S(1)} %pad_maximum_fusion.5), channel_id=1, source_target_pairs={{0,4},{4,0},{8,12},{12,8},{1,5},{5,1},{9,13},{13,9},{2,6},{6,2},{1... | collective-permute-start | bytes 3145736 | tf_op jit(solution)/shard_map/ppermute | solution.py:20
  119.7 11.8 %collective-permute-start.19 = (bf16[128,4096]{1,0:T(8,128)(2,1)S(1)}, bf16[128,4096]{1,0:T(8,128)(2,1)S(1)}, u32[]{:S(2)}, u32[]{:S(2)}) collective-permute-start(bf16[128,4096]{1,0:T(8,128)(2,1)S(1)} %pad_maximum_fusion.3), channel_id=1, source_target_pairs={{0,4},{4,0},{8,12},{12,8},{1,5},{5,1},{9,13},{13,9},{2,6},{6,2},{1... | collective-permute-start | bytes 3145736 | tf_op jit(solution)/shard_map/ppermute | solution.py:20
  127.0 27.7 %collective-permute-start.7 = (bf16[128,4096]{1,0:T(8,128)(2,1)}, bf16[128,4096]{1,0:T(8,128)(2,1)}, u32[]{:S(2)}, u32[]{:S(2)}) collective-permute-start(bf16[128,4096]{1,0:T(8,128)(2,1)} %pad_maximum_fusion.1), channel_id=1, source_target_pairs={{0,4},{4,0},{8,12},{12,8},{1,5},{5,1},{9,13},{13,9},{2,6},{6,2},{1... | collective-permute-start | bytes 3145736 | tf_op jit(solution)/shard_map/ppermute | solution.py:20
  128.2 40.8 %collective-permute-start.13 = (bf16[128,4096]{1,0:T(8,128)(2,1)}, bf16[128,4096]{1,0:T(8,128)(2,1)S(1)}, u32[]{:S(2)}, u32[]{:S(2)}) collective-permute-start(bf16[128,4096]{1,0:T(8,128)(2,1)} %pad_maximum_fusion.2), channel_id=1, source_target_pairs={{0,4},{4,0},{8,12},{12,8},{1,5},{5,1},{9,13},{13,9},{2,6},{6,2},{1... | collective-permute-start | bytes 3145736 | tf_op jit(solution)/shard_map/ppermute | solution.py:20
  131.6 8.5 %collective-permute-start.1 = (bf16[128,4096]{1,0:T(8,128)(2,1)}, bf16[128,4096]{1,0:T(8,128)(2,1)S(1)}, u32[]{:S(2)}, u32[]{:S(2)}) collective-permute-start(bf16[128,4096]{1,0:T(8,128)(2,1)} %pad_maximum_fusion), channel_id=1, source_target_pairs={{0,4},{4,0},{8,12},{12,8},{1,5},{5,1},{9,13},{13,9},{2,6},{6,2},{1... | collective-permute-start | bytes 3145736 | tf_op jit(solution)/shard_map/ppermute | solution.py:20
  135.1 116.1 %collective-permute-start.20 = (bf16[256,896]{1,0:T(8,128)(2,1)}, bf16[256,896]{1,0:T(8,128)(2,1)S(1)}, u32[]{:S(2)}, u32[]{:S(2)}) collective-permute-start(bf16[256,896]{1,0:T(8,128)(2,1)} %get-tuple-element.53), channel_id=1, source_target_pairs={{0,16},{16,0},{1,17},{17,1},{2,18},{18,2},{3,19},{19,3},{4,20},{20... | collective-permute-start | bytes 1376264 | tf_op jit(solution)/shard_map/ppermute | solution.py:20
  140.1 56.4 %collective-permute-start.30 = (bf16[256,896]{1,0:T(8,128)(2,1)}, bf16[256,896]{1,0:T(8,128)(2,1)}, u32[]{:S(2)}, u32[]{:S(2)}) collective-permute-start(bf16[256,896]{1,0:T(8,128)(2,1)} %get-tuple-element.41), channel_id=1, source_target_pairs={{0,16},{16,0},{1,17},{17,1},{2,18},{18,2},{3,19},{19,3},{4,20},{20... | collective-permute-start | bytes 1376264 | tf_op jit(solution)/shard_map/ppermute | solution.py:20
  185.1 41.4 %collective-permute-start.25 = (bf16[256,896]{1,0:T(8,128)(2,1)}, bf16[256,896]{1,0:T(8,128)(2,1)S(1)}, u32[]{:S(2)}, u32[]{:S(2)}) collective-permute-start(bf16[256,896]{1,0:T(8,128)(2,1)} %get-tuple-element.47), channel_id=1, source_target_pairs={{0,16},{16,0},{1,17},{17,1},{2,18},{18,2},{3,19},{19,3},{4,20},{20... | collective-permute-start | bytes 1376264 | tf_op jit(solution)/shard_map/ppermute | solution.py:20
  187.7 32.2 %copy-start.27 = (f32[256,896]{1,0:T(8,128)S(1)}, f32[256,896]{1,0:T(8,128)}, u32[]{:S(2)}) copy-start(f32[256,896]{1,0:T(8,128)} %get-tuple-element.42) | copy-start | bytes 2752516
  187.7 32.2 %copy-start.31 = (f32[256,896]{1,0:T(8,128)S(1)}, f32[256,896]{1,0:T(8,128)}, u32[]{:S(2)}) copy-start(f32[256,896]{1,0:T(8,128)} %get-tuple-element.46) | copy-start | bytes 2752516
  187.7 32.2 %copy-start.32 = (f32[256,896]{1,0:T(8,128)S(1)}, f32[256,896]{1,0:T(8,128)}, u32[]{:S(2)}) copy-start(f32[256,896]{1,0:T(8,128)} %get-tuple-element.44) | copy-start | bytes 2752516
  192.6 16.0 %collective-permute-start.15 = (bf16[256,896]{1,0:T(8,128)(2,1)S(1)}, bf16[256,896]{1,0:T(8,128)(2,1)S(1)}, u32[]{:S(2)}, u32[]{:S(2)}) collective-permute-start(bf16[256,896]{1,0:T(8,128)(2,1)S(1)} %copy-done.43), channel_id=1, source_target_pairs={{0,16},{16,0},{1,17},{17,1},{2,18},{18,2},{3,19},{19,3},{4,20},{20... | collective-permute-start | bytes 1376264 | tf_op jit(solution)/shard_map/ppermute | solution.py:20
  193.1 25.3 %collective-permute-start.14 = (bf16[256,896]{1,0:T(8,128)(2,1)S(1)}, bf16[256,896]{1,0:T(8,128)(2,1)S(1)}, u32[]{:S(2)}, u32[]{:S(2)}) collective-permute-start(bf16[256,896]{1,0:T(8,128)(2,1)S(1)} %get-tuple-element.43), channel_id=1, source_target_pairs={{0,16},{16,0},{1,17},{17,1},{2,18},{18,2},{3,19},{19,3},{4,20},{20... | collective-permute-start | bytes 1376264 | tf_op jit(solution)/shard_map/ppermute | solution.py:20
  196.5 54.7 %collective-permute-start.3 = (bf16[256,896]{1,0:T(8,128)(2,1)S(1)}, bf16[256,896]{1,0:T(8,128)(2,1)S(1)}, u32[]{:S(2)}, u32[]{:S(2)}) collective-permute-start(bf16[256,896]{1,0:T(8,128)(2,1)S(1)} %copy-done.40), channel_id=1, source_target_pairs={{0,16},{16,0},{1,17},{17,1},{2,18},{18,2},{3,19},{19,3},{4,20},{20... | collective-permute-start | bytes 1376264 | tf_op jit(solution)/shard_map/ppermute | solution.py:20
  208.6 29.5 %collective-permute-start.9 = (bf16[256,896]{1,0:T(8,128)(2,1)S(1)}, bf16[256,896]{1,0:T(8,128)(2,1)S(1)}, u32[]{:S(2)}, u32[]{:S(2)}) collective-permute-start(bf16[256,896]{1,0:T(8,128)(2,1)S(1)} %copy-done.42), channel_id=1, source_target_pairs={{0,16},{16,0},{1,17},{17,1},{2,18},{18,2},{3,19},{19,3},{4,20},{20... | collective-permute-start | bytes 1376264 | tf_op jit(solution)/shard_map/ppermute | solution.py:20
  218.4 29.5 %collective-permute-start.8 = (bf16[256,896]{1,0:T(8,128)(2,1)}, bf16[256,896]{1,0:T(8,128)(2,1)S(1)}, u32[]{:S(2)}, u32[]{:S(2)}) collective-permute-start(bf16[256,896]{1,0:T(8,128)(2,1)} %get-tuple-element.49), channel_id=1, source_target_pairs={{0,16},{16,0},{1,17},{17,1},{2,18},{18,2},{3,19},{19,3},{4,20},{20... | collective-permute-start | bytes 1376264 | tf_op jit(solution)/shard_map/ppermute | solution.py:20
  222.4 41.2 %copy-start.11 = (bf16[256,896]{1,0:T(8,128)(2,1)}, bf16[256,896]{1,0:T(8,128)(2,1)S(1)}, u32[]{:S(2)}) copy-start(bf16[256,896]{1,0:T(8,128)(2,1)S(1)} %get-tuple-element.16) | copy-start | bytes 1376260
  226.6 30.1 %collective-permute-start.2 = (bf16[256,896]{1,0:T(8,128)(2,1)S(1)}, bf16[256,896]{1,0:T(8,128)(2,1)S(1)}, u32[]{:S(2)}, u32[]{:S(2)}) collective-permute-start(bf16[256,896]{1,0:T(8,128)(2,1)S(1)} %copy-done.41), channel_id=1, source_target_pairs={{0,16},{16,0},{1,17},{17,1},{2,18},{18,2},{3,19},{19,3},{4,20},{20... | collective-permute-start | bytes 1376264 | tf_op jit(solution)/shard_map/ppermute | solution.py:20
  248.6 43.1 %copy-start.12 = (bf16[256,896]{1,0:T(8,128)(2,1)}, bf16[256,896]{1,0:T(8,128)(2,1)S(1)}, u32[]{:S(2)}) copy-start(bf16[256,896]{1,0:T(8,128)(2,1)S(1)} %get-tuple-element.13) | copy-start | bytes 1376260
  258.4 30.6 %copy-start.13 = (bf16[256,896]{1,0:T(8,128)(2,1)}, bf16[256,896]{1,0:T(8,128)(2,1)S(1)}, u32[]{:S(2)}) copy-start(bf16[256,896]{1,0:T(8,128)(2,1)S(1)} %get-tuple-element.10) | copy-start | bytes 1376260
  260.7 27.8 %collective-permute-start.4 = (bf16[128,4096]{1,0:T(8,128)(2,1)}, bf16[128,4096]{1,0:T(8,128)(2,1)}, u32[]{:S(2)}, u32[]{:S(2)}) collective-permute-start(bf16[128,4096]{1,0:T(8,128)(2,1)} %convolution_convert_fusion.2), channel_id=1, source_target_pairs={{0,4},{4,0},{8,12},{12,8},{1,5},{5,1},{9,13},{13,9},{2,6},{6,2},{1... | collective-permute-start | bytes 3145736 | tf_op jit(solution)/shard_map/ppermute | solution.py:20
  263.1 28.5 %collective-permute-start.10 = (bf16[128,4096]{1,0:T(8,128)(2,1)}, bf16[128,4096]{1,0:T(8,128)(2,1)}, u32[]{:S(2)}, u32[]{:S(2)}) collective-permute-start(bf16[128,4096]{1,0:T(8,128)(2,1)} %convolution_convert_fusion.1), channel_id=1, source_target_pairs={{0,4},{4,0},{8,12},{12,8},{1,5},{5,1},{9,13},{13,9},{2,6},{6,2},{1... | collective-permute-start | bytes 3145736 | tf_op jit(solution)/shard_map/ppermute | solution.py:20
  265.9 40.9 %collective-permute-start.16 = (bf16[128,4096]{1,0:T(8,128)(2,1)}, bf16[128,4096]{1,0:T(8,128)(2,1)}, u32[]{:S(2)}, u32[]{:S(2)}) collective-permute-start(bf16[128,4096]{1,0:T(8,128)(2,1)} %convolution_convert_fusion), channel_id=1, source_target_pairs={{0,4},{4,0},{8,12},{12,8},{1,5},{5,1},{9,13},{13,9},{2,6},{6,2},{1... | collective-permute-start | bytes 3145736 | tf_op jit(solution)/shard_map/ppermute | solution.py:20
  268.2 65.0 %collective-permute-start.26 = (bf16[128,4096]{1,0:T(8,128)(2,1)}, bf16[128,4096]{1,0:T(8,128)(2,1)}, u32[]{:S(2)}, u32[]{:S(2)}) collective-permute-start(bf16[128,4096]{1,0:T(8,128)(2,1)} %fusion.1), channel_id=1, source_target_pairs={{0,4},{4,0},{8,12},{12,8},{1,5},{5,1},{9,13},{13,9},{2,6},{6,2},{1... | collective-permute-start | bytes 3145736 | tf_op jit(solution)/shard_map/ppermute | solution.py:20
  286.0 37.1 %collective-permute-start.31 = (bf16[128,4096]{1,0:T(8,128)(2,1)}, bf16[128,4096]{1,0:T(8,128)(2,1)}, u32[]{:S(2)}, u32[]{:S(2)}) collective-permute-start(bf16[128,4096]{1,0:T(8,128)(2,1)} %fusion.2), channel_id=1, source_target_pairs={{0,4},{4,0},{8,12},{12,8},{1,5},{5,1},{9,13},{13,9},{2,6},{6,2},{1... | collective-permute-start | bytes 3145736 | tf_op jit(solution)/shard_map/ppermute | solution.py:20
  288.6 57.2 %collective-permute-start.21 = (bf16[128,4096]{1,0:T(8,128)(2,1)}, bf16[128,4096]{1,0:T(8,128)(2,1)}, u32[]{:S(2)}, u32[]{:S(2)}) collective-permute-start(bf16[128,4096]{1,0:T(8,128)(2,1)} %fusion), channel_id=1, source_target_pairs={{0,4},{4,0},{8,12},{12,8},{1,5},{5,1},{9,13},{13,9},{2,6},{6,2},{1... | collective-permute-start | bytes 3145736 | tf_op jit(solution)/shard_map/ppermute | solution.py:20
  291.7 13.9 %collective-permute-start.5 = (bf16[64,4096]{1,0:T(8,128)(2,1)S(1)}, bf16[64,4096]{1,0:T(8,128)(2,1)S(1)}, u32[]{:S(2)}, u32[]{:S(2)}) collective-permute-start(bf16[64,4096]{1,0:T(8,128)(2,1)S(1)} %slice.263), channel_id=1, source_target_pairs={{0,8},{4,12},{8,0},{12,4},{1,9},{5,13},{9,1},{13,5},{2,10},{6,14},... | collective-permute-start | bytes 1572872 | tf_op jit(solution)/shard_map/ppermute | solution.py:20
  305.6 15.2 %collective-permute-start.11 = (bf16[64,4096]{1,0:T(8,128)(2,1)}, bf16[64,4096]{1,0:T(8,128)(2,1)}, u32[]{:S(2)}, u32[]{:S(2)}) collective-permute-start(bf16[64,4096]{1,0:T(8,128)(2,1)} %slice.262), channel_id=1, source_target_pairs={{0,8},{4,12},{8,0},{12,4},{1,9},{5,13},{9,1},{13,5},{2,10},{6,14},... | collective-permute-start | bytes 1572872 | tf_op jit(solution)/shard_map/ppermute | solution.py:20
  306.8 75.1 %reduce-scatter.9.cloned.1.call-start = ((), (), s32[]{:S(2)}) async-start(), calls=%async_computation.7 | async-start | bytes 655360 | tf_op jit(solution)/shard_map/reduce_scatter | solution.py:59
  313.8 17.3 %collective-permute-start.17 = (bf16[64,4096]{1,0:T(8,128)(2,1)}, bf16[64,4096]{1,0:T(8,128)(2,1)}, u32[]{:S(2)}, u32[]{:S(2)}) collective-permute-start(bf16[64,4096]{1,0:T(8,128)(2,1)} %slice.261), channel_id=1, source_target_pairs={{0,8},{4,12},{8,0},{12,4},{1,9},{5,13},{9,1},{13,5},{2,10},{6,14},... | collective-permute-start | bytes 1572872 | tf_op jit(solution)/shard_map/ppermute | solution.py:20
  322.8 59.2 %reduce-scatter.11.cloned.1.call-start = ((), (), s32[]{:S(2)}) async-start(), calls=%async_computation.8 | async-start | bytes 655360 | tf_op jit(solution)/shard_map/reduce_scatter | solution.py:59
  330.8 12.8 %collective-permute-start.32 = (bf16[64,4096]{1,0:T(8,128)(2,1)}, bf16[64,4096]{1,0:T(8,128)(2,1)}, u32[]{:S(2)}, u32[]{:S(2)}) collective-permute-start(bf16[64,4096]{1,0:T(8,128)(2,1)} %slice.258), channel_id=1, source_target_pairs={{0,8},{4,12},{8,0},{12,4},{1,9},{5,13},{9,1},{13,5},{2,10},{6,14},... | collective-permute-start | bytes 1572872 | tf_op jit(solution)/shard_map/ppermute | solution.py:20
  333.2 62.9 %reduce-scatter.17.cloned.1.call-start = ((), (), s32[]{:S(2)}) async-start(), calls=%async_computation.11 | async-start | bytes 655360 | tf_op jit(solution)/shard_map/reduce_scatter | solution.py:59
  339.1 15.8 %collective-permute-start.27 = (bf16[64,4096]{1,0:T(8,128)(2,1)}, bf16[64,4096]{1,0:T(8,128)(2,1)}, u32[]{:S(2)}, u32[]{:S(2)}) collective-permute-start(bf16[64,4096]{1,0:T(8,128)(2,1)} %slice.259), channel_id=1, source_target_pairs={{0,8},{4,12},{8,0},{12,4},{1,9},{5,13},{9,1},{13,5},{2,10},{6,14},... | collective-permute-start | bytes 1572872 | tf_op jit(solution)/shard_map/ppermute | solution.py:20
  345.7 72.3 %reduce-scatter.15.cloned.1.call-start = ((), (), s32[]{:S(2)}) async-start(), calls=%async_computation.10 | async-start | bytes 655360 | tf_op jit(solution)/shard_map/reduce_scatter | solution.py:59
  351.5 16.8 %collective-permute-start.22 = (bf16[64,4096]{1,0:T(8,128)(2,1)}, bf16[64,4096]{1,0:T(8,128)(2,1)}, u32[]{:S(2)}, u32[]{:S(2)}) collective-permute-start(bf16[64,4096]{1,0:T(8,128)(2,1)} %slice.260), channel_id=1, source_target_pairs={{0,8},{4,12},{8,0},{12,4},{1,9},{5,13},{9,1},{13,5},{2,10},{6,14},... | collective-permute-start | bytes 1572872 | tf_op jit(solution)/shard_map/ppermute | solution.py:20
  356.9 83.0 %reduce-scatter.13.cloned.1.call-start = ((), (), s32[]{:S(2)}) async-start(), calls=%async_computation.9 | async-start | bytes 655360 | tf_op jit(solution)/shard_map/reduce_scatter | solution.py:59
  370.3 69.6 %copy-start.19 = (f32[1024,192]{0,1:T(8,128)S(1)}, f32[1024,192]{0,1:T(8,128)}, u32[]{:S(2)}) copy-start(f32[1024,192]{0,1:T(8,128)} %param.9) | copy-start | bytes 2359300
  (41 other events, 375.6 us)
Sparse Core Ops, SparseCore 0:
  306.9 21.4 reduce-scatter.6
  331.3 19.7 reduce-scatter.8
  353.9 19.9 reduce-scatter.10
  376.0 19.9 reduce-scatter.16
  398.2 19.7 reduce-scatter.14
  420.1 19.7 reduce-scatter.12

commit v2 on v1

v2 whole, which is shorter than its diff:
```python
import jax
import jax.numpy as jnp
from jax import lax
from jax.sharding import PartitionSpec as P

momentum = 0.5
BF = jnp.bfloat16
F32 = jnp.float32


def contract(left, right, left_dim, right_dim):
    return lax.dot_general(
        left, right, (((left_dim,), (right_dim,)), ((), ())), preferred_element_type=F32
    )


def swap(value, axis, mask):
    n = lax.axis_size(axis)
    return lax.ppermute(value, axis, [(i, i ^ mask) for i in range(n)])


def merge_cols(cols):
    n, t, f = cols.shape
    return cols.transpose(1, 0, 2).reshape(t, n * f)


def gather_cols(block):
    return merge_cols(lax.all_gather(block, "col", axis=0, tiled=False))


def with_sibling(value):
    return jnp.concatenate([value, swap(value, "row", 1)], axis=0)


def depth_sum(part):
    return depth_sum_and_got(part)[0]


def depth_sum_and_got(part):
    if lax.axis_size("depth") == 2:
        got = swap(part.astype(BF), "depth", 1)
        return part + got.astype(F32), got
    total = lax.psum(part, "depth")
    return total, total


def fold_sibling(term, rows):
    got = swap(term(rows // 2, rows).astype(BF), "row", 1)
    return term(0, rows // 2) + got.astype(F32)


def scatter_sum(near, far):
    total = near + swap(far.astype(BF), "row", 2).astype(F32)
    n = lax.axis_size("col")
    t, f = total.shape
    blocks = total.astype(BF).reshape(t, n, f // n).transpose(1, 0, 2)
    return lax.psum_scatter(blocks, "col", scatter_dimension=0, tiled=False).astype(F32).T


def nonlinear(gate, up_val, d_act):
    sig = jax.nn.sigmoid(gate)
    act = (gate * sig * up_val).astype(BF)
    d_act, _ = lax.optimization_barrier((d_act, act))
    d_gate = (d_act * up_val * sig * (1.0 + gate * (1.0 - sig))).astype(BF)
    d_up = (d_act * gate * sig).astype(BF)
    return (act, d_gate, d_up)


def on_device(x_out, v_out, dx_out, dv_out, gate_weight, up_weight, down_weight):
    x_prev = x_out - v_out
    x_tok = x_prev.astype(BF).T
    df_tok = ((1.0 - momentum) * (dx_out + dv_out)).astype(BF).T
    x_near = gather_cols(x_tok)
    df_cols = lax.all_gather(df_tok, "col", axis=0, tiled=False)
    x_far = swap(x_near, "row", 2)
    x_pair = with_sibling(x_near)
    gate_near, gate_got = depth_sum_and_got(contract(x_pair, gate_weight, 1, 1))
    up_near = depth_sum(contract(x_pair, up_weight, 1, 1))
    df_cols, _ = lax.optimization_barrier((df_cols, gate_got))
    df_near = merge_cols(df_cols)
    xs = (x_pair, with_sibling(x_far))
    dfs = (with_sibling(df_near), with_sibling(swap(df_near, "row", 2)))
    gates = [gate_near, depth_sum(contract(xs[1], gate_weight, 1, 1))]
    ups = [up_near, depth_sum(contract(xs[1], up_weight, 1, 1))]
    d_acts = [depth_sum(contract(df, down_weight, 1, 1)) for df in dfs]
    rows = xs[0].shape[0]
    acts, dgates, dups = [], [], []
    ys, dxs = [], []
    for gate, up_val, d_act in zip(gates, ups, d_acts):
        act, d_gate, d_up = nonlinear(gate, up_val, d_act)
        acts.append(act)
        dgates.append(d_gate)
        dups.append(d_up)

        def down_term(lo, hi, act=act):
            return contract(act[lo:hi], down_weight, 1, 0)

        def input_term(lo, hi, d_gate=d_gate, d_up=d_up):
            return contract(d_gate[lo:hi], gate_weight, 1, 0) + contract(
                d_up[lo:hi], up_weight, 1, 0
            )

        ys.append(fold_sibling(down_term, rows))
        dxs.append(fold_sibling(input_term, rows))
    y_out = scatter_sum(*ys)
    dx_sum = scatter_sum(*dxs)
    x_all, df_all = jnp.concatenate(xs, 0), jnp.concatenate(dfs, 0)
    grad_gate = contract(jnp.concatenate(dgates, 0), x_all, 0, 0)
    grad_up = contract(jnp.concatenate(dups, 0), x_all, 0, 0)
    grad_down = contract(jnp.concatenate(acts, 0), df_all, 0, 0)
    v_prev = (v_out - (1.0 - momentum) * y_out) / momentum
    dx_prev = dx_out + dx_sum
    return (x_prev, v_prev, dx_prev, grad_gate, grad_up, grad_down)


def solution(mesh):
    act_spec, weight_spec = P(("depth", "col"), "row"), P(("col", "row"), "depth")
    return jax.shard_map(
        on_device,
        mesh=mesh,
        in_specs=(act_spec,) * 4 + (weight_spec,) * 3,
        out_specs=(act_spec,) * 3 + (weight_spec,) * 3,
        check_vma=False,
    )
```

time: 454 us -> 322 us (0.71)
  blocking collectives: 97 us -> 0 us
  local copies, waits for them, and re-layouts: 39.8 us -> 21.5 us
  starting transfers between devices: 23.7 us -> 12 us
  matrix products: 124 us -> 114 us
  waiting for transfers between devices: 128 us -> 136 us
    all_gather x6 -> x0, blocking collectives: 97 us -> none  [gather_tokens(): cols = lax.all_gather(block, 'col', axis=0, tiled=False)]
    reduce_scatter x6 -> x2, waiting for transfers between devices: 55.9 us -> 0.01 us  [scatter_sum(): lax.psum_scatter(blocks, 'col', scatter_dimension=0, tiled=False)]
    all_gather x0 -> x2, waiting for transfers between devices: none -> 40.2 us  [the longest x1 40.2 us: gather_cols(): return merge_cols(lax.all_gather(block, 'col', axis=0, tiled=False))]
    ppermute x33 -> x18, waiting for transfers between devices: 71.7 us -> 96 us  [swap(): return lax.ppermute(value, axis, [(i, i ^ mask) for i in range(n)])]
    unnamed x122 -> x79, local copies, waits for them, and re-layouts: 25.2 us -> 10.4 us
    ppermute x33 -> x18, starting transfers between devices: 23.2 us -> 11.7 us  [swap(): return lax.ppermute(value, axis, [(i, i ^ mask) for i in range(n)])]
    dot_general x30 -> x21, matrix products: 124 us -> 114 us  [contract(): lax.dot_general(left, right, (((left_dim,), (right_dim,)), ((), ())), pre...]
  transfers between devices with their start and end apart: 39 -> 22, of which waited for: 13 -> 8; matrix products, arithmetic and copies ran while one was open for 38% -> 46% of each run, Pallas kernels for 0% -> 0%
where the time goes in v2:
time: 322 us; the launch traced here: 318 us
  waiting for transfers between devices  136 us (42%)
  matrix products  114 us (35%)
  local copies, waits for them, and re-layouts  21.5 us (7%)
  other arithmetic  20.2 us (6%)
  between operations  14.4 us (4%)
  starting transfers between devices  12 us (4%)
    dot_general x21, matrix products, contract(): lax.dot_general(left, right, (((left_dim,), (right_dim,)), ((), ())), pre...  114 us
    ppermute x18, waiting for transfers between devices, swap(): return lax.ppermute(value, axis, [(i, i ^ mask) for i in range(n)])  96 us
    all_gather x1, waiting for transfers between devices, gather_cols(): return merge_cols(lax.all_gather(block, 'col', axis=0, tiled=False))  40.2 us
    ppermute x18, starting transfers between devices, swap(): return lax.ppermute(value, axis, [(i, i ^ mask) for i in range(n)])  11.7 us
    unnamed x79, local copies, waits for them, and re-layouts  10.4 us
  transfers between devices with their start and end apart: 22, of which 8 were waited for; matrix products, arithmetic and copies ran while one was open for 46% of the time, Pallas kernels for 0%

profile of v2, /device:TPU:0, one launch (start us, length us, event | category | flops | bytes accessed | tf_op | source)
XLA Modules:
  0.0 317.8 jit_solution(10282840551392134073)
XLA Ops:
  7.2 2.5 convert_bitcast_fusion.1
  9.8 40.2 %all-gather.5.cloned.1.call-done = bf16[768,1024]{1,0:T(8,128)(2,1)} async-done(((bf16[192,1024]{1,0:T(8,128)(2,1)}), bf16[768,1024]{1,0:T(8,128)(2,1)}) %all-gather.5.cloned.1.call-update) | async-done | bytes 1572880 | tf_op jit(solution)/shard_map/all_gather | solution.py:28
  50.0 2.7 copy.15
  54.4 1.5 collective-permute-start.4
  58.7 8.4 %fusion.62 = (bf16[384,896]{1,0:T(8,128)(2,1)}, f32[384,896]{1,0:T(8,128)}) fusion(bf16[384,4096]{1,0:T(8,128)(2,1)S(1)} %get-tuple-element.23, bf16[896,4096]{1,0:T(8,128)(2,1)} %param.11), kind=kOutput, calls=%fused_computation.96 | convolution fusion | flops 2818916352 | bytes 12550144 | tf_op jit(solution)/shard_map/dot_general | solution.py:12
  68.6 4.7 %fusion.61 = (bf16[384,896]{1,0:T(8,128)(2,1)}, f32[384,896]{1,0:T(8,128)}) fusion(bf16[384,4096]{1,0:T(8,128)(2,1)S(1)} %get-tuple-element.23, bf16[896,4096]{1,0:T(8,128)(2,1)S(1)} %bitcast.66), kind=kOutput, calls=%fused_computation.95 | convolution fusion | flops 2818916352 | bytes 12550144 | tf_op jit(solution)/shard_map/dot_general | solution.py:12
  74.0 17.3 %collective-permute-done.4 = bf16[192,4096]{1,0:T(8,128)(2,1)} collective-permute-done((bf16[192,4096]{1,0:T(8,128)(2,1)S(1)}, bf16[192,4096]{1,0:T(8,128)(2,1)}, u32[]{:S(2)}, u32[]{:S(2)}) %collective-permute-start.4) | collective-permute-done | bytes 1572896 | tf_op jit(solution)/shard_map/ppermute | solution.py:19
  91.4 3.6 %constant_dynamic-update-slice_fusion.5 = (bf16[768,4096]{1,0:T(8,128)(2,1)}, bf16[384,4096]{1,0:T(8,128)(2,1)}) fusion(bf16[768,4096]{1,0:T(8,128)(2,1)} %get-tuple-element.22, bf16[192,4096]{1,0:T(8,128)(2,1)} %collective-permute-done.4), kind=kLoop, calls=%fused_computation.85 | loop fusion | bytes 4718592
  95.0 2.8 copy.17
  97.8 1.9 copy.22
  99.6 1.5 collective-permute-start.13
  101.3 1.8 multiply_convert_fusion.5
  103.2 3.0 convolution_convert_fusion.1
  106.6 3.6 %fusion.52 = f32[192,4096]{1,0:T(8,128)} fusion(bf16[896,4096]{1,0:T(8,128)(2,1)S(1)} %bitcast.70, bf16[384,896]{1,0:T(8,128)(2,1)S(1)} %multiply_convert_fusion.5), kind=kOutput, calls=%fused_computation.78 | convolution fusion | flops 1409286144 | bytes 10829824 | tf_op jit(solution)/shard_map/dot_general | solution.py:12
  110.1 3.0 constant_dynamic-update-slice_fusion.4
  113.1 4.5 %fusion.60 = (bf16[384,896]{1,0:T(8,128)(2,1)}, f32[384,896]{1,0:T(8,128)S(1)}) fusion(bf16[384,4096]{1,0:T(8,128)(2,1)S(1)} %get-tuple-element.19, bf16[896,4096]{1,0:T(8,128)(2,1)S(1)} %bitcast.64), kind=kOutput, calls=%fused_computation.94 | convolution fusion | flops 2818916352 | bytes 12550144 | tf_op jit(solution)/shard_map/dot_general | solution.py:12
  117.6 1.5 collective-permute-start.6
  119.1 4.8 %fusion.59 = (bf16[384,896]{1,0:T(8,128)(2,1)}, f32[384,896]{1,0:T(8,128)}) fusion(bf16[384,4096]{1,0:T(8,128)(2,1)S(1)} %get-tuple-element.19, bf16[896,4096]{1,0:T(8,128)(2,1)S(1)} %bitcast.68), kind=kOutput, calls=%fused_computation.93 | convolution fusion | flops 2818916352 | bytes 12550144 | tf_op jit(solution)/shard_map/dot_general | solution.py:12
  124.4 6.6 %fusion.64 = (bf16[384,896]{1,0:T(8,128)(2,1)}, f32[384,896]{1,0:T(8,128)}) fusion(bf16[896,4096]{1,0:T(8,128)(2,1)S(1)} %bitcast.70, bf16[192,4096]{1,0:T(8,128)(2,1)} %collective-permute-done.10, bf16[192,4096]{1,0:T(8,128)(2,1)} %bitcast.21), kind=kOutput, calls=%fused_computation.98 | convolution fusion | flops 2825207808 | bytes 12550144 | tf_op jit(solution)/shard_map/dot_general | solution.py:12
  131.0 1.5 collective-permute-start.11
  132.5 4.2 %collective-permute-done.13 = bf16[192,4096]{1,0:T(8,128)(2,1)} collective-permute-done((bf16[192,4096]{1,0:T(8,128)(2,1)}, bf16[192,4096]{1,0:T(8,128)(2,1)}, u32[]{:S(2)}, u32[]{:S(2)}) %collective-permute-start.13) | collective-permute-done | bytes 1572896 | tf_op jit(solution)/shard_map/ppermute | solution.py:19
  136.8 14.2 %collective-permute-done.7 = bf16[384,896]{1,0:T(8,128)(2,1)} collective-permute-done((bf16[384,896]{1,0:T(8,128)(2,1)}, bf16[384,896]{1,0:T(8,128)(2,1)}, u32[]{:S(2)}, u32[]{:S(2)}) %collective-permute-start.7) | collective-permute-done | bytes 688160 | tf_op jit(solution)/shard_map/ppermute | solution.py:19
  151.0 2.2 multiply_convert_fusion.4
  154.0 3.0 convolution_convert_fusion
  157.1 7.8 %collective-permute-done.11 = bf16[384,896]{1,0:T(8,128)(2,1)S(1)} collective-permute-done((bf16[384,896]{1,0:T(8,128)(2,1)}, bf16[384,896]{1,0:T(8,128)(2,1)S(1)}, u32[]{:S(2)}, u32[]{:S(2)}) %collective-permute-start.11) | collective-permute-done | bytes 688160 | tf_op jit(solution)/shard_map/ppermute | solution.py:19
  165.1 2.1 multiply_convert_fusion.2
  167.2 3.5 %fusion.41 = f32[192,4096]{1,0:T(8,128)} fusion(bf16[896,4096]{1,0:T(8,128)(2,1)S(1)} %bitcast.64, bf16[384,896]{1,0:T(8,128)(2,1)S(1)} %get-tuple-element.15), kind=kOutput, calls=%fused_computation.69 | convolution fusion | flops 1409286144 | bytes 10829824 | tf_op jit(solution)/shard_map/dot_general | solution.py:12
  170.7 7.0 %fusion.63 = (bf16[384,896]{1,0:T(8,128)(2,1)}, f32[384,896]{1,0:T(8,128)}) fusion(bf16[896,4096]{1,0:T(8,128)(2,1)S(1)} %bitcast.70, bf16[192,4096]{1,0:T(8,128)(2,1)} %collective-permute-done.14, bf16[192,4096]{1,0:T(8,128)(2,1)} %collective-permute-done.13), kind=kOutput, calls=%fused_computation.97 | convolution fusion | flops 2825207808 | bytes 12550144 | tf_op jit(solution)/shard_map/dot_general | solution.py:12
  177.7 1.5 collective-permute-start.15
  179.2 5.0 %fusion.8 = bf16[192,4096]{1,0:T(8,128)(2,1)} fusion(f32[192,4096]{1,0:T(8,128)} %fusion.41, bf16[896,4096]{1,0:T(8,128)(2,1)S(1)} %bitcast.68, bf16[384,896]{1,0:T(8,128)(2,1)S(1)} %get-tuple-element.14), kind=kOutput, calls=%fused_computation.12 | convolution fusion | flops 1410859008 | bytes 12402688 | tf_op jit(solution)/shard_map/dot_general | solution.py:12
  184.3 3.3 %add_convert_fusion.3 = bf16[192,4096]{1,0:T(8,128)(2,1)S(1)} fusion(bf16[192,4096]{1,0:T(8,128)(2,1)} %collective-permute-done.8, bf16[896,4096]{1,0:T(8,128)(2,1)S(1)} %bitcast.70, bf16[384,896]{1,0:T(8,128)(2,1)S(1)} %copy-done.27), kind=kOutput, calls=%fused_computation.27 | convolution fusion | flops 1411645440 | bytes 10829824 | tf_op jit(solution)/shard_map/dot_general | solution.py:12
  188.3 6.4 %collective-permute-done.15 = bf16[384,896]{1,0:T(8,128)(2,1)S(1)} collective-permute-done((bf16[384,896]{1,0:T(8,128)(2,1)}, bf16[384,896]{1,0:T(8,128)(2,1)S(1)}, u32[]{:S(2)}, u32[]{:S(2)}) %collective-permute-start.15) | collective-permute-done | bytes 688160 | tf_op jit(solution)/shard_map/ppermute | solution.py:19
  194.9 2.1 multiply_convert_fusion
  197.0 1.8 fusion.33
  198.8 3.1 fusion.9
  202.0 1.8 fusion.38
  203.8 20.6 %collective-permute-done.9 = bf16[192,4096]{1,0:T(8,128)(2,1)S(1)} collective-permute-done((bf16[192,4096]{1,0:T(8,128)(2,1)S(1)}, bf16[192,4096]{1,0:T(8,128)(2,1)S(1)}, u32[]{:S(2)}, u32[]{:S(2)}) %collective-permute-start.9) | collective-permute-done | bytes 1572896 | tf_op jit(solution)/shard_map/ppermute | solution.py:19
  224.4 2.1 add_convert_fusion.2
  228.1 5.8 %add_convert_fusion.1 = bf16[192,4096]{1,0:T(8,128)(2,1)S(1)} fusion(bf16[192,4096]{1,0:T(8,128)(2,1)} %collective-permute-done.16, f32[192,4096]{1,0:T(8,128)S(1)} %fusion.38, bf16[896,4096]{1,0:T(8,128)(2,1)} %param.12, bf16[384,896]{1,0:T(8,128)(2,1)} %copy-done.8), kind=kOutput, calls=%fused_computation.25 | convolution fusion | flops 1412431872 | bytes 13975552 | tf_op jit(solution)/shard_map/dot_general | solution.py:12
  234.2 5.0 %fusion.44 = f32[192,4096]{1,0:T(8,128)S(1)} fusion(bf16[896,4096]{1,0:T(8,128)(2,1)} %param.11, bf16[384,896]{1,0:T(8,128)(2,1)S(1)} %copy-done.2), kind=kOutput, calls=%fused_computation.72 | convolution fusion | flops 1409286144 | bytes 10829824 | tf_op jit(solution)/shard_map/dot_general | solution.py:12
  239.2 4.9 %convolution_add_fusion.3 = f32[192,4096]{1,0:T(8,128)S(1)} fusion(f32[192,4096]{1,0:T(8,128)S(1)} %fusion.44, bf16[896,4096]{1,0:T(8,128)(2,1)} %param.12, bf16[384,896]{1,0:T(8,128)(2,1)S(1)} %copy-done.7), kind=kOutput, calls=%fused_computation.11 | convolution fusion | flops 1410072576 | bytes 13975552 | tf_op jit(solution)/shard_map/dot_general | solution.py:12
  244.1 25.4 %collective-permute-done.17 = bf16[192,4096]{1,0:T(8,128)(2,1)S(1)} collective-permute-done((bf16[192,4096]{1,0:T(8,128)(2,1)S(1)}, bf16[192,4096]{1,0:T(8,128)(2,1)S(1)}, u32[]{:S(2)}, u32[]{:S(2)}) %collective-permute-start.17) | collective-permute-done | bytes 1572896 | tf_op jit(solution)/shard_map/ppermute | solution.py:19
  269.5 2.0 add_convert_fusion
  273.4 11.1 %fusion = f32[896,4096]{1,0:T(8,128)} fusion(bf16[192,4096]{1,0:T(8,128)(2,1)} %collective-permute-done.14, bf16[192,4096]{1,0:T(8,128)(2,1)} %collective-permute-done.13, bf16[192,4096]{1,0:T(8,128)(2,1)} %collective-permute-done.10, bf16[192,4096]{1,0:T(8,128)(2,1)} %bitcast.21, bf16[384,896]{1,0:T(8,128)(2,1)S(1)} %copy-done.28, ...), kind=kOutput, calls=%fused_computation | convolution fusion | flops 5665062912 | bytes 22347776 | tf_op jit(solution)/shard_map/dot_general | solution.py:12
  284.6 11.2 %fusion.22 = f32[896,4096]{1,0:T(8,128)} fusion(bf16[768,4096]{1,0:T(8,128)(2,1)} %get-tuple-element.18, bf16[384,896]{1,0:T(8,128)(2,1)S(1)} %copy-done.9, bf16[384,896]{1,0:T(8,128)(2,1)S(1)} %copy-done.7), kind=kOutput, calls=%fused_computation.34 | convolution fusion | flops 5639897088 | bytes 22347776 | tf_op jit(solution)/shard_map/dot_general | solution.py:12
  295.8 11.3 %fusion.18 = f32[896,4096]{1,0:T(8,128)} fusion(bf16[768,4096]{1,0:T(8,128)(2,1)} %get-tuple-element.18, bf16[384,896]{1,0:T(8,128)(2,1)S(1)} %copy-done.5, bf16[384,896]{1,0:T(8,128)(2,1)S(1)} %copy-done.3), kind=kOutput, calls=%fused_computation.30 | convolution fusion | flops 5639897088 | bytes 22347776 | tf_op jit(solution)/shard_map/dot_general | solution.py:12
  307.1 2.0 fusion.30
  309.1 2.0 fusion.29
  (121 shorter events, 13.4 us)
Async XLA Ops:
  7.2 42.8 %all-gather.5.cloned.1.call-start = ((), (), s32[]{:S(2)}) async-start(), calls=%async_computation.4 | async-start | bytes 1966080 | tf_op jit(solution)/shard_map/all_gather | solution.py:28
  9.8 85.2 %all-gather.7.cloned.1.call-start = ((), (), s32[]{:S(2)}) async-start(), calls=%async_computation.5 | async-start | bytes 1966080 | tf_op jit(solution)/shard_map/all_gather | solution.py:74
  53.3 4.0 %collective-permute-start = (bf16[192,4096]{1,0:T(8,128)(2,1)S(1)}, bf16[192,4096]{1,0:T(8,128)(2,1)S(1)}, u32[]{:S(2)}, u32[]{:S(2)}) collective-permute-start(bf16[192,4096]{1,0:T(8,128)(2,1)S(1)} %bitcast.75), channel_id=1, source_target_pairs={{0,4},{4,0},{8,12},{12,8},{1,5},{5,1},{9,13},{13,9},{2,6},{6,2},{1... | collective-permute-start | bytes 4718600 | tf_op jit(solution)/shard_map/ppermute | solution.py:19
  54.4 252.7 %reduce-scatter.3.cloned.1.call-start = ((), (), s32[]{:S(2)}) async-start(), calls=%async_computation.2 | async-start | bytes 1966080 | tf_op jit(solution)/shard_map/reduce_scatter | solution.py:57
  54.4 37.0 %collective-permute-start.4 = (bf16[192,4096]{1,0:T(8,128)(2,1)S(1)}, bf16[192,4096]{1,0:T(8,128)(2,1)}, u32[]{:S(2)}, u32[]{:S(2)}) collective-permute-start(bf16[192,4096]{1,0:T(8,128)(2,1)S(1)} %bitcast.76), channel_id=1, source_target_pairs={{0,8},{4,12},{8,0},{12,4},{1,9},{5,13},{9,1},{13,5},{2,10},{6,14},... | collective-permute-start | bytes 4718600 | tf_op jit(solution)/shard_map/ppermute | solution.py:19
  57.3 11.3 %slice-start.2 = ((s8[7340032]{0:T(1024)(128)(4,1)}), s8[4194304]{0:T(1024)(128)(4,1)S(1)}, s32[]{:S(2)}) async-start(s8[7340032]{0:T(1024)(128)(4,1)} %bitcast.65), calls=%async_computation.8 | async-start | bytes 8388608
  58.7 9.9 %slice-start.3 = ((s8[7340032]{0:T(1024)(128)(4,1)}), s8[3145728]{0:T(1024)(128)(4,1)S(1)}, s32[]{:S(2)}) async-start(s8[7340032]{0:T(1024)(128)(4,1)} %bitcast.65), calls=%async_computation.9 | async-start | bytes 6291456
  67.2 27.8 %collective-permute-start.1 = (bf16[384,896]{1,0:T(8,128)(2,1)}, bf16[384,896]{1,0:T(8,128)(2,1)}, u32[]{:S(2)}, u32[]{:S(2)}) collective-permute-start(bf16[384,896]{1,0:T(8,128)(2,1)} %get-tuple-element.32), channel_id=1, source_target_pairs={{0,16},{16,0},{1,17},{17,1},{2,18},{18,2},{3,19},{19,3},{4,20},{20... | collective-permute-start | bytes 2064392 | tf_op jit(solution)/shard_map/ppermute | solution.py:19
  73.4 28.0 %collective-permute-start.2 = (bf16[384,896]{1,0:T(8,128)(2,1)}, bf16[384,896]{1,0:T(8,128)(2,1)}, u32[]{:S(2)}, u32[]{:S(2)}) collective-permute-start(bf16[384,896]{1,0:T(8,128)(2,1)} %get-tuple-element.30), channel_id=1, source_target_pairs={{0,16},{16,0},{1,17},{17,1},{2,18},{18,2},{3,19},{19,3},{4,20},{20... | collective-permute-start | bytes 2064392 | tf_op jit(solution)/shard_map/ppermute | solution.py:19
  91.4 18.8 %collective-permute-start.5 = (bf16[192,4096]{1,0:T(8,128)(2,1)}, bf16[192,4096]{1,0:T(8,128)(2,1)}, u32[]{:S(2)}, u32[]{:S(2)}) collective-permute-start(bf16[192,4096]{1,0:T(8,128)(2,1)} %collective-permute-done.4), channel_id=1, source_target_pairs={{0,4},{4,0},{8,12},{12,8},{1,5},{5,1},{9,13},{13,9},{2,6},{6,2},{1... | collective-permute-start | bytes 4718600 | tf_op jit(solution)/shard_map/ppermute | solution.py:19
  91.4 11.8 %slice-start.6 = ((s8[7340032]{0:T(1024)(128)(4,1)}), s8[3145728]{0:T(1024)(128)(4,1)S(1)}, s32[]{:S(2)}) async-start(s8[7340032]{0:T(1024)(128)(4,1)} %bitcast.69), calls=%async_computation.12 | async-start | bytes 6291456
  95.0 6.4 %copy-start.10 = (f32[384,896]{1,0:T(8,128)S(1)}, f32[384,896]{1,0:T(8,128)}, u32[]{:S(2)}) copy-start(f32[384,896]{1,0:T(8,128)} %get-tuple-element.33) | copy-start | bytes 4128772
  95.0 6.4 %copy-start.12 = (f32[384,896]{1,0:T(8,128)S(1)}, f32[384,896]{1,0:T(8,128)}, u32[]{:S(2)}) copy-start(f32[384,896]{1,0:T(8,128)} %get-tuple-element.31) | copy-start | bytes 4128772
  97.8 5.4 %slice-start.7 = ((s8[7340032]{0:T(1024)(128)(4,1)}), s8[4194304]{0:T(1024)(128)(4,1)S(1)}, s32[]{:S(2)}) async-start(s8[7340032]{0:T(1024)(128)(4,1)} %bitcast.69), calls=%async_computation.13 | async-start | bytes 8388608
  99.6 37.1 %collective-permute-start.13 = (bf16[192,4096]{1,0:T(8,128)(2,1)}, bf16[192,4096]{1,0:T(8,128)(2,1)}, u32[]{:S(2)}, u32[]{:S(2)}) collective-permute-start(bf16[192,4096]{1,0:T(8,128)(2,1)} %bitcast.21), channel_id=1, source_target_pairs={{0,8},{4,12},{8,0},{12,4},{1,9},{5,13},{9,1},{13,5},{2,10},{6,14},... | collective-permute-start | bytes 4718600 | tf_op jit(solution)/shard_map/ppermute | solution.py:19
  101.1 23.3 %collective-permute-start.10 = (bf16[192,4096]{1,0:T(8,128)(2,1)}, bf16[192,4096]{1,0:T(8,128)(2,1)}, u32[]{:S(2)}, u32[]{:S(2)}) collective-permute-start(bf16[192,4096]{1,0:T(8,128)(2,1)} %bitcast.21), channel_id=1, source_target_pairs={{0,4},{4,0},{8,12},{12,8},{1,5},{5,1},{9,13},{13,9},{2,6},{6,2},{1... | collective-permute-start | bytes 4718600 | tf_op jit(solution)/shard_map/ppermute | solution.py:19
  103.2 9.9 %slice-start = ((s8[7340032]{0:T(1024)(128)(4,1)}), s8[4194304]{0:T(1024)(128)(4,1)S(1)}, s32[]{:S(2)}) async-start(s8[7340032]{0:T(1024)(128)(4,1)} %bitcast.63), calls=%async_computation.6 | async-start | bytes 8388608
  106.3 6.8 %slice-start.1 = ((s8[7340032]{0:T(1024)(128)(4,1)}), s8[3145728]{0:T(1024)(128)(4,1)S(1)}, s32[]{:S(2)}) async-start(s8[7340032]{0:T(1024)(128)(4,1)} %bitcast.63), calls=%async_computation.7 | async-start | bytes 6291456
  106.3 97.5 %collective-permute-start.3 = (bf16[192,4096]{1,0:T(8,128)(2,1)}, bf16[192,4096]{1,0:T(8,128)(2,1)}, u32[]{:S(2)}, u32[]{:S(2)}) collective-permute-start(bf16[192,4096]{1,0:T(8,128)(2,1)} %convolution_convert_fusion.1), channel_id=1, source_target_pairs={{0,4},{4,0},{8,12},{12,8},{1,5},{5,1},{9,13},{13,9},{2,6},{6,2},{1... | collective-permute-start | bytes 4718600 | tf_op jit(solution)/shard_map/ppermute | solution.py:19
  110.1 9.0 %slice-start.4 = ((s8[7340032]{0:T(1024)(128)(4,1)}), s8[4194304]{0:T(1024)(128)(4,1)S(1)}, s32[]{:S(2)}) async-start(s8[7340032]{0:T(1024)(128)(4,1)} %bitcast.67), calls=%async_computation.10 | async-start | bytes 8388608
  113.1 6.0 %slice-start.5 = ((s8[7340032]{0:T(1024)(128)(4,1)}), s8[3145728]{0:T(1024)(128)(4,1)S(1)}, s32[]{:S(2)}) async-start(s8[7340032]{0:T(1024)(128)(4,1)} %bitcast.67), calls=%async_computation.11 | async-start | bytes 6291456
  117.6 33.3 %copy-start.14 = (f32[384,896]{1,0:T(8,128)}, f32[384,896]{1,0:T(8,128)S(1)}, u32[]{:S(2)}) copy-start(f32[384,896]{1,0:T(8,128)S(1)} %get-tuple-element.29) | copy-start | bytes 4128772
  117.6 19.1 %collective-permute-start.6 = (bf16[384,896]{1,0:T(8,128)(2,1)}, bf16[384,896]{1,0:T(8,128)(2,1)}, u32[]{:S(2)}, u32[]{:S(2)}) collective-permute-start(bf16[384,896]{1,0:T(8,128)(2,1)} %get-tuple-element.28), channel_id=1, source_target_pairs={{0,16},{16,0},{1,17},{17,1},{2,18},{18,2},{3,19},{19,3},{4,20},{20... | collective-permute-start | bytes 2064392 | tf_op jit(solution)/shard_map/ppermute | solution.py:19
  123.8 27.1 %collective-permute-start.7 = (bf16[384,896]{1,0:T(8,128)(2,1)}, bf16[384,896]{1,0:T(8,128)(2,1)}, u32[]{:S(2)}, u32[]{:S(2)}) collective-permute-start(bf16[384,896]{1,0:T(8,128)(2,1)} %get-tuple-element.26), channel_id=1, source_target_pairs={{0,16},{16,0},{1,17},{17,1},{2,18},{18,2},{3,19},{19,3},{4,20},{20... | collective-permute-start | bytes 2064392 | tf_op jit(solution)/shard_map/ppermute | solution.py:19
  131.0 33.9 %collective-permute-start.11 = (bf16[384,896]{1,0:T(8,128)(2,1)}, bf16[384,896]{1,0:T(8,128)(2,1)S(1)}, u32[]{:S(2)}, u32[]{:S(2)}) collective-permute-start(bf16[384,896]{1,0:T(8,128)(2,1)} %get-tuple-element.36), channel_id=1, source_target_pairs={{0,16},{16,0},{1,17},{17,1},{2,18},{18,2},{3,19},{19,3},{4,20},{20... | collective-permute-start | bytes 2064392 | tf_op jit(solution)/shard_map/ppermute | solution.py:19
  136.7 33.9 %collective-permute-start.14 = (bf16[192,4096]{1,0:T(8,128)(2,1)}, bf16[192,4096]{1,0:T(8,128)(2,1)}, u32[]{:S(2)}, u32[]{:S(2)}) collective-permute-start(bf16[192,4096]{1,0:T(8,128)(2,1)} %collective-permute-done.13), channel_id=1, source_target_pairs={{0,4},{4,0},{8,12},{12,8},{1,5},{5,1},{9,13},{13,9},{2,6},{6,2},{1... | collective-permute-start | bytes 4718600 | tf_op jit(solution)/shard_map/ppermute | solution.py:19
  154.0 10.9 %copy-start.22 = (f32[384,896]{1,0:T(8,128)S(1)}, f32[384,896]{1,0:T(8,128)}, u32[]{:S(2)}) copy-start(f32[384,896]{1,0:T(8,128)} %get-tuple-element.37) | copy-start | bytes 4128772
  157.1 8.0 %copy-start.11 = (f32[384,896]{1,0:T(8,128)S(1)}, f32[384,896]{1,0:T(8,128)}, u32[]{:S(2)}) copy-start(f32[384,896]{1,0:T(8,128)} %get-tuple-element.33) | copy-start | bytes 4128772
  157.1 8.0 %copy-start.13 = (f32[384,896]{1,0:T(8,128)S(1)}, f32[384,896]{1,0:T(8,128)}, u32[]{:S(2)}) copy-start(f32[384,896]{1,0:T(8,128)} %get-tuple-element.31) | copy-start | bytes 4128772
  157.1 27.2 %collective-permute-start.8 = (bf16[192,4096]{1,0:T(8,128)(2,1)}, bf16[192,4096]{1,0:T(8,128)(2,1)}, u32[]{:S(2)}, u32[]{:S(2)}) collective-permute-start(bf16[192,4096]{1,0:T(8,128)(2,1)} %convolution_convert_fusion), channel_id=1, source_target_pairs={{0,4},{4,0},{8,12},{12,8},{1,5},{5,1},{9,13},{13,9},{2,6},{6,2},{1... | collective-permute-start | bytes 4718600 | tf_op jit(solution)/shard_map/ppermute | solution.py:19
  167.2 12.0 %copy-start.6 = (bf16[384,896]{1,0:T(8,128)(2,1)}, bf16[384,896]{1,0:T(8,128)(2,1)S(1)}, u32[]{:S(2)}) copy-start(bf16[384,896]{1,0:T(8,128)(2,1)S(1)} %get-tuple-element.14) | copy-start | bytes 2064388
  177.7 17.0 %collective-permute-start.15 = (bf16[384,896]{1,0:T(8,128)(2,1)}, bf16[384,896]{1,0:T(8,128)(2,1)S(1)}, u32[]{:S(2)}, u32[]{:S(2)}) collective-permute-start(bf16[384,896]{1,0:T(8,128)(2,1)} %get-tuple-element.34), channel_id=1, source_target_pairs={{0,16},{16,0},{1,17},{17,1},{2,18},{18,2},{3,19},{19,3},{4,20},{20... | collective-permute-start | bytes 2064392 | tf_op jit(solution)/shard_map/ppermute | solution.py:19
  184.2 10.4 %copy-start.23 = (f32[384,896]{1,0:T(8,128)S(1)}, f32[384,896]{1,0:T(8,128)}, u32[]{:S(2)}) copy-start(f32[384,896]{1,0:T(8,128)} %get-tuple-element.35) | copy-start | bytes 4128772
  184.3 59.9 %collective-permute-start.12 = (bf16[192,4096]{1,0:T(8,128)(2,1)}, bf16[192,4096]{1,0:T(8,128)(2,1)}, u32[]{:S(2)}, u32[]{:S(2)}) collective-permute-start(bf16[192,4096]{1,0:T(8,128)(2,1)} %fusion.8), channel_id=1, source_target_pairs={{0,4},{4,0},{8,12},{12,8},{1,5},{5,1},{9,13},{13,9},{2,6},{6,2},{1... | collective-permute-start | bytes 4718600 | tf_op jit(solution)/shard_map/ppermute | solution.py:19
  187.6 7.3 %copy-start.15 = (f32[384,896]{1,0:T(8,128)S(1)}, f32[384,896]{1,0:T(8,128)}, u32[]{:S(2)}) copy-start(f32[384,896]{1,0:T(8,128)} %copy-done.14) | copy-start | bytes 4128772
  187.6 7.3 %copy-start.16 = (f32[384,896]{1,0:T(8,128)S(1)}, f32[384,896]{1,0:T(8,128)}, u32[]{:S(2)}) copy-start(f32[384,896]{1,0:T(8,128)} %get-tuple-element.27) | copy-start | bytes 4128772
  187.6 36.8 %collective-permute-start.9 = (bf16[192,4096]{1,0:T(8,128)(2,1)S(1)}, bf16[192,4096]{1,0:T(8,128)(2,1)S(1)}, u32[]{:S(2)}, u32[]{:S(2)}) collective-permute-start(bf16[192,4096]{1,0:T(8,128)(2,1)S(1)} %add_convert_fusion.3), channel_id=1, source_target_pairs={{0,8},{4,12},{8,0},{12,4},{1,9},{5,13},{9,1},{13,5},{2,10},{6,14},... | collective-permute-start | bytes 4718600 | tf_op jit(solution)/shard_map/ppermute | solution.py:19
  202.0 22.4 %copy-start = (f32[192,4096]{1,0:T(8,128)S(1)}, f32[192,4096]{1,0:T(8,128)}, u32[]{:S(2)}) copy-start(f32[192,4096]{1,0:T(8,128)} %fusion.52) | copy-start | bytes 9437188
  202.0 26.1 %collective-permute-start.16 = (bf16[192,4096]{1,0:T(8,128)(2,1)}, bf16[192,4096]{1,0:T(8,128)(2,1)}, u32[]{:S(2)}, u32[]{:S(2)}) collective-permute-start(bf16[192,4096]{1,0:T(8,128)(2,1)} %fusion.9), channel_id=1, source_target_pairs={{0,4},{4,0},{8,12},{12,8},{1,5},{5,1},{9,13},{13,9},{2,6},{6,2},{1... | collective-permute-start | bytes 4718600 | tf_op jit(solution)/shard_map/ppermute | solution.py:19
  227.8 81.3 %reduce-scatter.5.cloned.1.call-start = ((), (), s32[]{:S(2)}) async-start(), calls=%async_computation.3 | async-start | bytes 1966080 | tf_op jit(solution)/shard_map/reduce_scatter | solution.py:57
  228.1 6.2 %copy-start.2 = (bf16[384,896]{1,0:T(8,128)(2,1)S(1)}, bf16[384,896]{1,0:T(8,128)(2,1)}, u32[]{:S(2)}) copy-start(bf16[384,896]{1,0:T(8,128)(2,1)} %copy-done.1) | copy-start | bytes 2064388
  233.9 5.3 %copy-start.7 = (bf16[384,896]{1,0:T(8,128)(2,1)S(1)}, bf16[384,896]{1,0:T(8,128)(2,1)}, u32[]{:S(2)}) copy-start(bf16[384,896]{1,0:T(8,128)(2,1)} %copy-done.6) | copy-start | bytes 2064388
  233.9 35.7 %collective-permute-start.17 = (bf16[192,4096]{1,0:T(8,128)(2,1)S(1)}, bf16[192,4096]{1,0:T(8,128)(2,1)S(1)}, u32[]{:S(2)}, u32[]{:S(2)}) collective-permute-start(bf16[192,4096]{1,0:T(8,128)(2,1)S(1)} %add_convert_fusion.1), channel_id=1, source_target_pairs={{0,8},{4,12},{8,0},{12,4},{1,9},{5,13},{9,1},{13,5},{2,10},{6,14},... | collective-permute-start | bytes 4718600 | tf_op jit(solution)/shard_map/ppermute | solution.py:19
  273.4 11.1 %copy-start.9 = (bf16[384,896]{1,0:T(8,128)(2,1)S(1)}, bf16[384,896]{1,0:T(8,128)(2,1)}, u32[]{:S(2)}) copy-start(bf16[384,896]{1,0:T(8,128)(2,1)} %copy-done.8) | copy-start | bytes 2064388
  284.5 11.2 %copy-start.3 = (bf16[384,896]{1,0:T(8,128)(2,1)S(1)}, bf16[384,896]{1,0:T(8,128)(2,1)}, u32[]{:S(2)}) copy-start(bf16[384,896]{1,0:T(8,128)(2,1)} %copy-done.1) | copy-start | bytes 2064388
  284.5 11.2 %copy-start.5 = (bf16[384,896]{1,0:T(8,128)(2,1)S(1)}, bf16[384,896]{1,0:T(8,128)(2,1)}, u32[]{:S(2)}) copy-start(bf16[384,896]{1,0:T(8,128)(2,1)} %copy-done.4) | copy-start | bytes 2064388
  295.8 11.3 %copy-start.17 = (f32[1024,192]{0,1:T(8,128)S(1)}, f32[1024,192]{0,1:T(8,128)}, u32[]{:S(2)}) copy-start(f32[1024,192]{0,1:T(8,128)} %param.8) | copy-start | bytes 2359300
  295.8 13.3 %copy-start.19 = (f32[1024,192]{0,1:T(8,128)S(1)}, f32[1024,192]{0,1:T(8,128)}, u32[]{:S(2)}) copy-start(f32[1024,192]{0,1:T(8,128)} %param.9) | copy-start | bytes 2359300
  (11 other events, 33.5 us)
Sparse Core Ops, SparseCore 0:
  10.1 39.7 all-gather.4
  54.5 36.0 all-gather.6
  228.0 32.3 reduce-scatter.2
  273.0 32.3 reduce-scatter.4

commit v3 on v2

v3 whole, which is shorter than its diff:
```python
import jax
import jax.numpy as jnp
from jax import lax
from jax.sharding import PartitionSpec as P

momentum = 0.5
BF = jnp.bfloat16
F32 = jnp.float32


def contract(left, right, left_dim, right_dim):
    return lax.dot_general(
        left, right, (((left_dim,), (right_dim,)), ((), ())), preferred_element_type=F32
    )


def swap(value, axis, mask):
    n = lax.axis_size(axis)
    return lax.ppermute(value, axis, [(i, i ^ mask) for i in range(n)])


def merge_cols(cols):
    n, t, f = cols.shape
    return cols.transpose(1, 0, 2).reshape(t, n * f)


def gather_cols(block):
    return merge_cols(lax.all_gather(block, "col", axis=0, tiled=False))


def with_sibling(value):
    return jnp.concatenate([value, swap(value, "row", 1)], axis=0)


def depth_sum(part):
    return depth_sum_and_got(part)[0]


def depth_sum_and_got(part):
    if lax.axis_size("depth") == 2:
        got = swap(part.astype(BF), "depth", 1)
        return part + got.astype(F32), got
    total = lax.psum(part, "depth")
    return total, total


def fold_sibling(term, rows):
    got = swap(term(rows // 2, rows).astype(BF), "row", 1)
    return term(0, rows // 2) + got.astype(F32)


def scatter_sum(near, got):
    total = near + got.astype(F32)
    n = lax.axis_size("col")
    t, f = total.shape
    blocks = total.astype(BF).reshape(t, n, f // n).transpose(1, 0, 2)
    return lax.psum_scatter(blocks, "col", scatter_dimension=0, tiled=False).astype(F32).T


def after(value, earlier):
    return lax.optimization_barrier((value, earlier))[0]


def activation(gate, up_val):
    return (gate * jax.nn.sigmoid(gate) * up_val).astype(BF)


def cotangents(gate, up_val, d_act):
    sig = jax.nn.sigmoid(gate)
    d_gate = (d_act * up_val * sig * (1.0 + gate * (1.0 - sig))).astype(BF)
    d_up = (d_act * gate * sig).astype(BF)
    return (d_gate, d_up)


def on_device(x_out, v_out, dx_out, dv_out, gate_weight, up_weight, down_weight):
    x_prev = x_out - v_out
    x_tok = x_prev.astype(BF).T
    df_tok = ((1.0 - momentum) * (dx_out + dv_out)).astype(BF).T
    x_near = gather_cols(x_tok)
    df_cols = lax.all_gather(df_tok, "col", axis=0, tiled=False)
    x_far = swap(x_near, "row", 2)
    xa = with_sibling(x_near)
    gate_a, gate_got = depth_sum_and_got(contract(xa, gate_weight, 1, 1))
    up_a = depth_sum(contract(xa, up_weight, 1, 1))
    df_near = merge_cols(after(df_cols, gate_got))
    df_far = swap(df_near, "row", 2)
    xb, dfa, dfb = with_sibling(x_far), with_sibling(df_near), with_sibling(df_far)
    gate_b = depth_sum(contract(xb, gate_weight, 1, 1))
    up_b_part = contract(xb, up_weight, 1, 1)
    up_b = depth_sum(up_b_part)
    dact_a_part = contract(dfa, down_weight, 1, 1)
    dact_a = depth_sum(dact_a_part)
    dact_b_part = contract(dfb, down_weight, 1, 1)
    dact_b = depth_sum(dact_b_part)
    rows = xa.shape[0]

    def down_fold(act):
        return fold_sibling(lambda lo, hi: contract(act[lo:hi], down_weight, 1, 0), rows)

    def input_fold(d_gate, d_up):
        return fold_sibling(
            lambda lo, hi: contract(d_gate[lo:hi], gate_weight, 1, 0)
            + contract(d_up[lo:hi], up_weight, 1, 0),
            rows,
        )

    act_a = activation(gate_a, up_a)
    y_near = down_fold(after(after(act_a, up_b_part), dact_a_part))
    act_b = activation(gate_b, up_b)
    y_got = swap(down_fold(after(act_b, dact_b_part)).astype(BF), "row", 2)
    dgate_b, dup_b = cotangents(gate_b, up_b, after(dact_b, act_b))
    dx_far = input_fold(dgate_b, dup_b).astype(BF)
    dx_got = swap(dx_far, "row", 2)
    y_out = scatter_sum(y_near, after(y_got, dx_far))
    dgate_a, dup_a = cotangents(gate_a, up_a, after(dact_a, act_a))
    dx_near = input_fold(after(dgate_a, dx_far), dup_a)
    dx_sum = scatter_sum(dx_near, dx_got)
    xs, dfs = (xa, xb), (dfa, dfb)
    acts, dgates, dups = (act_a, act_b), (dgate_a, dgate_b), (dup_a, dup_b)
    x_all = after(jnp.concatenate(xs, 0), dx_far)
    df_all = after(jnp.concatenate(dfs, 0), dx_far)
    grad_gate = contract(jnp.concatenate(dgates, 0), x_all, 0, 0)
    grad_up = contract(jnp.concatenate(dups, 0), x_all, 0, 0)
    grad_down = contract(jnp.concatenate(acts, 0), df_all, 0, 0)
    v_prev = (v_out - (1.0 - momentum) * y_out) / momentum
    dx_prev = dx_out + dx_sum
    return (x_prev, v_prev, dx_prev, grad_gate, grad_up, grad_down)


def solution(mesh):
    act_spec, weight_spec = P(("depth", "col"), "row"), P(("col", "row"), "depth")
    return jax.shard_map(
        on_device,
        mesh=mesh,
        in_specs=(act_spec,) * 4 + (weight_spec,) * 3,
        out_specs=(act_spec,) * 3 + (weight_spec,) * 3,
        check_vma=False,
    )
```

time: 322 us -> 326 us (1.012)
  other arithmetic: 20.2 us -> 36.2 us
  matrix products: 114 us -> 105 us
  local copies, waits for them, and re-layouts: 21.5 us -> 18 us
    concatenate x0 -> x2, other arithmetic: none -> 12.3 us  [the longest x1 6.48 us: on_device(): df_all = after(jnp.concatenate(dfs, 0), dx_far)]
    dot_general x21, matrix products: 114 us -> 105 us  [contract(): lax.dot_general(left, right, (((left_dim,), (right_dim,)), ((), ())), pre...]
    ppermute x18, waiting for transfers between devices: 96 us -> 89.2 us  [swap(): return lax.ppermute(value, axis, [(i, i ^ mask) for i in range(n)])]
    unnamed x79 -> x92, local copies, waits for them, and re-layouts: 10.4 us -> 5.2 us
    reduce_scatter x2, waiting for transfers between devices: 0.01 us -> 4.83 us  [scatter_sum(): lax.psum_scatter(blocks, 'col', scatter_dimension=0, tiled=False)]
  transfers between devices with their start and end apart: 22 -> 22, of which waited for: 8 -> 9; matrix products, arithmetic and copies ran while one was open for 46% -> 47% of each run, Pallas kernels for 0% -> 0%
where the time goes in v3:
time: 326 us; the launch traced here: 322 us
  waiting for transfers between devices  134 us (41%)
  matrix products  105 us (32%)
  other arithmetic  36.2 us (11%)
  local copies, waits for them, and re-layouts  18 us (6%)
  between operations  14.6 us (4%)
  starting transfers between devices  14.1 us (4%)
    dot_general x21, matrix products, contract(): lax.dot_general(left, right, (((left_dim,), (right_dim,)), ((), ())), pre...  105 us
    ppermute x18, waiting for transfers between devices, swap(): return lax.ppermute(value, axis, [(i, i ^ mask) for i in range(n)])  89.2 us
    all_gather x1, waiting for transfers between devices, gather_cols(): return merge_cols(lax.all_gather(block, 'col', axis=0, tiled=False))  40.2 us
    ppermute x18, starting transfers between devices, swap(): return lax.ppermute(value, axis, [(i, i ^ mask) for i in range(n)])  13.5 us
  transfers between devices with their start and end apart: 22, of which 9 were waited for; matrix products, arithmetic and copies ran while one was open for 47% of the time, Pallas kernels for 0%

profile of v3, /device:TPU:0, one launch (start us, length us, event | category | flops | bytes accessed | tf_op | source)
XLA Modules:
  0.0 321.6 jit_solution(2753003636361913101)
XLA Ops:
  7.2 2.5 convert_bitcast_fusion.1
  9.8 40.2 %all-gather.5.cloned.1.call-done = bf16[768,1024]{1,0:T(8,128)(2,1)} async-done(((bf16[192,1024]{1,0:T(8,128)(2,1)}), bf16[768,1024]{1,0:T(8,128)(2,1)}) %all-gather.5.cloned.1.call-update) | async-done | bytes 1572880 | tf_op jit(solution)/shard_map/all_gather | solution.py:28
  50.0 2.7 copy.15
  54.4 1.5 collective-permute-start.3
  57.0 1.7 constant_dynamic-update-slice_fusion
  58.6 7.7 %fusion.54 = (bf16[384,896]{1,0:T(8,128)(2,1)}, f32[384,896]{1,0:T(8,128)S(1)}) fusion(bf16[384,4096]{1,0:T(8,128)(2,1)S(1)} %constant_dynamic-update-slice_fusion, bf16[896,4096]{1,0:T(8,128)(2,1)} %param.11), kind=kOutput, calls=%fused_computation.86 | convolution fusion | flops 2818916352 | bytes 12550144 | tf_op jit(solution)/shard_map/dot_general | solution.py:12
  67.8 23.6 %collective-permute-done.3 = bf16[192,4096]{1,0:T(8,128)(2,1)} collective-permute-done((bf16[192,4096]{1,0:T(8,128)(2,1)S(1)}, bf16[192,4096]{1,0:T(8,128)(2,1)}, u32[]{:S(2)}, u32[]{:S(2)}) %collective-permute-start.3) | collective-permute-done | bytes 1572896 | tf_op jit(solution)/shard_map/ppermute | solution.py:19
  91.4 4.7 %fusion.56 = (bf16[384,896]{1,0:T(8,128)(2,1)}, f32[384,896]{1,0:T(8,128)}) fusion(bf16[384,4096]{1,0:T(8,128)(2,1)S(1)} %constant_dynamic-update-slice_fusion, bf16[896,4096]{1,0:T(8,128)(2,1)S(1)} %bitcast.69), kind=kOutput, calls=%fused_computation.88 | convolution fusion | flops 2818916352 | bytes 12550144 | tf_op jit(solution)/shard_map/dot_general | solution.py:12
  97.6 2.7 constant_dynamic-update-slice_fusion.3
  100.3 2.8 copy.16
  103.7 1.5 collective-permute-start.9
  105.3 9.0 %collective-permute-done.2 = bf16[384,896]{1,0:T(8,128)(2,1)} collective-permute-done((bf16[384,896]{1,0:T(8,128)(2,1)}, bf16[384,896]{1,0:T(8,128)(2,1)}, u32[]{:S(2)}, u32[]{:S(2)}) %collective-permute-start.2) | collective-permute-done | bytes 688160 | tf_op jit(solution)/shard_map/ppermute | solution.py:19
  114.3 2.8 multiply_convert_fusion.5
  117.1 2.9 constant_dynamic-update-slice_fusion.2
  120.0 7.0 %fusion.53 = (bf16[384,896]{1,0:T(8,128)(2,1)}, f32[384,896]{1,0:T(8,128)}) fusion(bf16[384,4096]{1,0:T(8,128)(2,1)} %constant_dynamic-update-slice_fusion.2, bf16[896,4096]{1,0:T(8,128)(2,1)S(1)} %bitcast.65), kind=kOutput, calls=%fused_computation.85 | convolution fusion | flops 2818916352 | bytes 12550144 | tf_op jit(solution)/shard_map/dot_general | solution.py:12
  128.5 6.9 %fusion.52 = (bf16[384,896]{1,0:T(8,128)(2,1)}, f32[384,896]{1,0:T(8,128)}) fusion(bf16[384,4096]{1,0:T(8,128)(2,1)} %constant_dynamic-update-slice_fusion.2, bf16[896,4096]{1,0:T(8,128)(2,1)S(1)} %bitcast.71), kind=kOutput, calls=%fused_computation.84 | convolution fusion | flops 2818916352 | bytes 12550144 | tf_op jit(solution)/shard_map/dot_general | solution.py:12
  136.3 5.8 %pad_maximum_fusion = bf16[768,4096]{1,0:T(8,128)(2,1)} fusion(bf16[192,4096]{1,0:T(8,128)(2,1)} %collective-permute-done.4, bf16[192,4096]{1,0:T(8,128)(2,1)} %collective-permute-done.3, bf16[192,4096]{1,0:T(8,128)(2,1)} %collective-permute-done, bf16[192,4096]{1,0:T(8,128)(2,1)S(1)} %bitcast.83), kind=kLoop, calls=%fused_computation | loop fusion | flops 25165824 | bytes 12582912 | tf_op jit(solution)/shard_map/concatenate | solution.py:120
  142.2 6.9 %fusion.57 = (bf16[384,896]{1,0:T(8,128)(2,1)}, f32[384,896]{1,0:T(8,128)}) fusion(bf16[896,4096]{1,0:T(8,128)(2,1)S(1)} %bitcast.79, bf16[192,4096]{1,0:T(8,128)(2,1)} %collective-permute-done.5, bf16[192,4096]{1,0:T(8,128)(2,1)} %bitcast.86), kind=kOutput, calls=%fused_computation.89 | convolution fusion | flops 2825207808 | bytes 12550144 | tf_op jit(solution)/shard_map/dot_general | solution.py:12
  150.4 2.9 convolution_convert_fusion.1
  153.5 7.0 %collective-permute-done.8 = bf16[384,896]{1,0:T(8,128)(2,1)} collective-permute-done((bf16[384,896]{1,0:T(8,128)(2,1)}, bf16[384,896]{1,0:T(8,128)(2,1)}, u32[]{:S(2)}, u32[]{:S(2)}) %collective-permute-start.8) | collective-permute-done | bytes 688160 | tf_op jit(solution)/shard_map/ppermute | solution.py:19
  160.5 2.7 multiply_convert_fusion.4
  163.1 3.5 %fusion.45 = f32[192,4096]{1,0:T(8,128)} fusion(bf16[896,4096]{1,0:T(8,128)(2,1)S(1)} %bitcast.79, bf16[384,896]{1,0:T(8,128)(2,1)S(1)} %copy-done.19), kind=kOutput, calls=%fused_computation.73 | convolution fusion | flops 1409286144 | bytes 10829824 | tf_op jit(solution)/shard_map/dot_general | solution.py:12
  166.6 6.6 %fusion.55 = (bf16[384,896]{1,0:T(8,128)(2,1)S(1)}, f32[384,896]{1,0:T(8,128)}) fusion(bf16[896,4096]{1,0:T(8,128)(2,1)S(1)} %bitcast.79, bf16[192,4096]{1,0:T(8,128)(2,1)} %collective-permute-done.10, bf16[192,4096]{1,0:T(8,128)(2,1)} %collective-permute-done.9), kind=kOutput, calls=%fused_computation.87 | convolution fusion | flops 2825207808 | bytes 12550144 | tf_op jit(solution)/shard_map/dot_general | solution.py:12
  174.7 1.6 convert_add_fusion
  176.4 3.0 convolution_convert_fusion
  179.3 9.2 %collective-permute-done.13 = bf16[384,896]{1,0:T(8,128)(2,1)S(1)} collective-permute-done((bf16[384,896]{1,0:T(8,128)(2,1)S(1)}, bf16[384,896]{1,0:T(8,128)(2,1)S(1)}, u32[]{:S(2)}, u32[]{:S(2)}) %collective-permute-start.13) | collective-permute-done | bytes 688160 | tf_op jit(solution)/shard_map/ppermute | solution.py:19
  188.7 2.1 multiply_convert_fusion.2
  190.8 2.0 fusion.28
  192.9 1.9 fusion
  194.9 3.0 multiply_convert_fusion
  197.9 3.5 %add_convert_fusion.3 = bf16[192,4096]{1,0:T(8,128)(2,1)S(1)} fusion(bf16[192,4096]{1,0:T(8,128)(2,1)} %collective-permute-done.11, bf16[896,4096]{1,0:T(8,128)(2,1)S(1)} %bitcast.79, bf16[384,896]{1,0:T(8,128)(2,1)S(1)} %copy-done.24), kind=kOutput, calls=%fused_computation.21 | convolution fusion | flops 1411645440 | bytes 10829824 | tf_op jit(solution)/shard_map/dot_general | solution.py:12
  202.9 1.8 fusion.33
  204.7 3.0 add_convert_fusion.2
  208.3 3.5 %fusion.35 = f32[192,4096]{1,0:T(8,128)} fusion(bf16[896,4096]{1,0:T(8,128)(2,1)S(1)} %bitcast.65, bf16[384,896]{1,0:T(8,128)(2,1)S(1)} %get-tuple-element.23), kind=kOutput, calls=%fused_computation.65 | convolution fusion | flops 1409286144 | bytes 10829824 | tf_op jit(solution)/shard_map/dot_general | solution.py:12
  211.7 26.9 %collective-permute-done.12 = bf16[192,4096]{1,0:T(8,128)(2,1)S(1)} collective-permute-done((bf16[192,4096]{1,0:T(8,128)(2,1)S(1)}, bf16[192,4096]{1,0:T(8,128)(2,1)S(1)}, u32[]{:S(2)}, u32[]{:S(2)}) %collective-permute-start.12) | collective-permute-done | bytes 1572896 | tf_op jit(solution)/shard_map/ppermute | solution.py:19
  238.6 2.1 add_convert_fusion.1
  242.6 6.0 %fusion.1 = bf16[192,4096]{1,0:T(8,128)(2,1)S(1)} fusion(f32[192,4096]{1,0:T(8,128)} %fusion.35, bf16[896,4096]{1,0:T(8,128)(2,1)} %param.12, bf16[384,896]{1,0:T(8,128)(2,1)} %get-tuple-element.28), kind=kOutput, calls=%fused_computation.7 | convolution fusion | flops 1410859008 | bytes 12402688 | tf_op jit(solution)/shard_map/dot_general | solution.py:12
  248.7 6.5 %pad_maximum_fusion.1 = bf16[768,4096]{1,0:T(8,128)(2,1)} fusion(bf16[192,4096]{1,0:T(8,128)(2,1)} %collective-permute-done.10, bf16[192,4096]{1,0:T(8,128)(2,1)} %collective-permute-done.9, bf16[192,4096]{1,0:T(8,128)(2,1)} %collective-permute-done.5, bf16[192,4096]{1,0:T(8,128)(2,1)S(1)} %bitcast.87), kind=kLoop, calls=%fused_computation.1 | loop fusion | flops 25165824 | bytes 12582912 | tf_op jit(solution)/shard_map/concatenate | solution.py:121
  255.3 1.8 fusion.37
  257.6 1.8 convolution_add_fusion.1
  259.4 12.6 %collective-permute-done.17 = bf16[192,4096]{1,0:T(8,128)(2,1)} collective-permute-done((bf16[192,4096]{1,0:T(8,128)(2,1)}, bf16[192,4096]{1,0:T(8,128)(2,1)}, u32[]{:S(2)}, u32[]{:S(2)}) %collective-permute-start.17) | collective-permute-done | bytes 1572896 | tf_op jit(solution)/shard_map/ppermute | solution.py:19
  272.0 2.0 add_convert_fusion
  276.0 11.2 %fusion.14 = f32[896,4096]{1,0:T(8,128)} fusion(bf16[768,4096]{1,0:T(8,128)(2,1)} %pad_maximum_fusion, bf16[384,896]{1,0:T(8,128)(2,1)S(1)} %copy-done.9, bf16[384,896]{1,0:T(8,128)(2,1)S(1)} %copy-done.7), kind=kOutput, calls=%fused_computation.28 | convolution fusion | flops 5639897088 | bytes 22347776 | tf_op jit(solution)/shard_map/dot_general | solution.py:12
  287.3 9.3 %fusion.10 = f32[896,4096]{1,0:T(8,128)} fusion(bf16[768,4096]{1,0:T(8,128)(2,1)S(1)} %bitcast.75, bf16[384,896]{1,0:T(8,128)(2,1)S(1)} %copy-done.2, bf16[384,896]{1,0:T(8,128)(2,1)S(1)} %copy-done.5), kind=kOutput, calls=%fused_computation.24 | convolution fusion | flops 5639897088 | bytes 22347776 | tf_op jit(solution)/shard_map/dot_general | solution.py:12
  296.6 9.5 %fusion.18 = f32[896,4096]{1,0:T(8,128)} fusion(bf16[768,4096]{1,0:T(8,128)(2,1)S(1)} %bitcast.77, bf16[384,896]{1,0:T(8,128)(2,1)S(1)} %copy-done.25, bf16[384,896]{1,0:T(8,128)(2,1)S(1)} %copy-done.20), kind=kOutput, calls=%fused_computation.32 | convolution fusion | flops 5639897088 | bytes 22347776 | tf_op jit(solution)/shard_map/dot_general | solution.py:12
  306.0 2.0 fusion.23
  308.1 4.8 %reduce-scatter.5.cloned.1.call-done = bf16[1,192,1024]{2,1,0:T(8,128)(2,1)} async-done(((bf16[4,192,1024]{2,1,0:T(8,128)(2,1)}), bf16[1,192,1024]{2,1,0:T(8,128)(2,1)}) %reduce-scatter.5.cloned.1.call-update) | async-done | bytes 393232 | tf_op jit(solution)/shard_map/reduce_scatter | solution.py:57
  312.9 2.0 fusion.22
  (141 shorter events, 18.2 us)
Async XLA Ops:
  7.2 42.8 %all-gather.5.cloned.1.call-start = ((), (), s32[]{:S(2)}) async-start(), calls=%async_computation.4 | async-start | bytes 1966080 | tf_op jit(solution)/shard_map/all_gather | solution.py:28
  9.8 90.5 %all-gather.7.cloned.1.call-start = ((), (), s32[]{:S(2)}) async-start(), calls=%async_computation.5 | async-start | bytes 1966080 | tf_op jit(solution)/shard_map/all_gather | solution.py:80
  53.3 3.6 %collective-permute-start = (bf16[192,4096]{1,0:T(8,128)(2,1)S(1)}, bf16[192,4096]{1,0:T(8,128)(2,1)}, u32[]{:S(2)}, u32[]{:S(2)}) collective-permute-start(bf16[192,4096]{1,0:T(8,128)(2,1)S(1)} %bitcast.80), channel_id=1, source_target_pairs={{0,4},{4,0},{8,12},{12,8},{1,5},{5,1},{9,13},{13,9},{2,6},{6,2},{1... | collective-permute-start | bytes 4718600 | tf_op jit(solution)/shard_map/ppermute | solution.py:19
  54.4 251.7 %reduce-scatter.3.cloned.1.call-start = ((), (), s32[]{:S(2)}) async-start(), calls=%async_computation.2 | async-start | bytes 1966080 | tf_op jit(solution)/shard_map/reduce_scatter | solution.py:57
  54.4 37.0 %collective-permute-start.3 = (bf16[192,4096]{1,0:T(8,128)(2,1)S(1)}, bf16[192,4096]{1,0:T(8,128)(2,1)}, u32[]{:S(2)}, u32[]{:S(2)}) collective-permute-start(bf16[192,4096]{1,0:T(8,128)(2,1)S(1)} %bitcast.81), channel_id=1, source_target_pairs={{0,8},{4,12},{8,0},{12,4},{1,9},{5,13},{9,1},{13,5},{2,10},{6,14},... | collective-permute-start | bytes 4718600 | tf_op jit(solution)/shard_map/ppermute | solution.py:19
  56.9 34.4 %slice-start.4 = ((s8[7340032]{0:T(1024)(128)(4,1)}), s8[4194304]{0:T(1024)(128)(4,1)S(1)}, s32[]{:S(2)}) async-start(s8[7340032]{0:T(1024)(128)(4,1)} %bitcast.68), calls=%async_computation.10 | async-start | bytes 8388608
  58.6 32.7 %slice-start.5 = ((s8[7340032]{0:T(1024)(128)(4,1)}), s8[3145728]{0:T(1024)(128)(4,1)S(1)}, s32[]{:S(2)}) async-start(s8[7340032]{0:T(1024)(128)(4,1)} %bitcast.68), calls=%async_computation.11 | async-start | bytes 6291456
  66.3 48.0 %copy-start.12 = (f32[384,896]{1,0:T(8,128)}, f32[384,896]{1,0:T(8,128)S(1)}, u32[]{:S(2)}) copy-start(f32[384,896]{1,0:T(8,128)S(1)} %get-tuple-element.37) | copy-start | bytes 4128772
  66.3 34.0 %collective-permute-start.1 = (bf16[384,896]{1,0:T(8,128)(2,1)}, bf16[384,896]{1,0:T(8,128)(2,1)}, u32[]{:S(2)}, u32[]{:S(2)}) collective-permute-start(bf16[384,896]{1,0:T(8,128)(2,1)} %get-tuple-element.36), channel_id=1, source_target_pairs={{0,16},{16,0},{1,17},{17,1},{2,18},{18,2},{3,19},{19,3},{4,20},{20... | collective-permute-start | bytes 2064392 | tf_op jit(solution)/shard_map/ppermute | solution.py:19
  91.4 25.8 %collective-permute-start.4 = (bf16[192,4096]{1,0:T(8,128)(2,1)}, bf16[192,4096]{1,0:T(8,128)(2,1)}, u32[]{:S(2)}, u32[]{:S(2)}) collective-permute-start(bf16[192,4096]{1,0:T(8,128)(2,1)} %collective-permute-done.3), channel_id=1, source_target_pairs={{0,4},{4,0},{8,12},{12,8},{1,5},{5,1},{9,13},{13,9},{2,6},{6,2},{1... | collective-permute-start | bytes 4718600 | tf_op jit(solution)/shard_map/ppermute | solution.py:19
  96.1 18.2 %collective-permute-start.2 = (bf16[384,896]{1,0:T(8,128)(2,1)}, bf16[384,896]{1,0:T(8,128)(2,1)}, u32[]{:S(2)}, u32[]{:S(2)}) collective-permute-start(bf16[384,896]{1,0:T(8,128)(2,1)} %get-tuple-element.40), channel_id=1, source_target_pairs={{0,16},{16,0},{1,17},{17,1},{2,18},{18,2},{3,19},{19,3},{4,20},{20... | collective-permute-start | bytes 2064392 | tf_op jit(solution)/shard_map/ppermute | solution.py:19
  100.3 14.0 %copy-start.14 = (f32[384,896]{1,0:T(8,128)S(1)}, f32[384,896]{1,0:T(8,128)}, u32[]{:S(2)}) copy-start(f32[384,896]{1,0:T(8,128)} %get-tuple-element.41) | copy-start | bytes 4128772
  100.3 19.7 %slice-start = ((s8[7340032]{0:T(1024)(128)(4,1)}), s8[4194304]{0:T(1024)(128)(4,1)S(1)}, s32[]{:S(2)}) async-start(s8[7340032]{0:T(1024)(128)(4,1)} %bitcast.64), calls=%async_computation.6 | async-start | bytes 8388608
  103.7 16.3 %copy-start.10 = (bf16[24,8,4,1024]{3,1,2,0:T(8,128)(2,1)}, bf16[24,8,4,1024]{3,1,2,0:T(8,128)(2,1)S(1)}, u32[]{:S(2)}) copy-start(bf16[24,8,4,1024]{3,1,2,0:T(8,128)(2,1)S(1)} %copy.22) | copy-start | bytes 4718596
  103.7 38.4 %collective-permute-start.9 = (bf16[192,4096]{1,0:T(8,128)(2,1)S(1)}, bf16[192,4096]{1,0:T(8,128)(2,1)}, u32[]{:S(2)}, u32[]{:S(2)}) collective-permute-start(bf16[192,4096]{1,0:T(8,128)(2,1)S(1)} %bitcast.84), channel_id=1, source_target_pairs={{0,8},{4,12},{8,0},{12,4},{1,9},{5,13},{9,1},{13,5},{2,10},{6,14},... | collective-permute-start | bytes 4718600 | tf_op jit(solution)/shard_map/ppermute | solution.py:19
  105.3 37.0 %collective-permute-start.5 = (bf16[192,4096]{1,0:T(8,128)(2,1)S(1)}, bf16[192,4096]{1,0:T(8,128)(2,1)}, u32[]{:S(2)}, u32[]{:S(2)}) collective-permute-start(bf16[192,4096]{1,0:T(8,128)(2,1)S(1)} %bitcast.85), channel_id=1, source_target_pairs={{0,4},{4,0},{8,12},{12,8},{1,5},{5,1},{9,13},{13,9},{2,6},{6,2},{1... | collective-permute-start | bytes 4718600 | tf_op jit(solution)/shard_map/ppermute | solution.py:19
  117.1 11.4 %slice-start.6 = ((s8[7340032]{0:T(1024)(128)(4,1)}), s8[4194304]{0:T(1024)(128)(4,1)S(1)}, s32[]{:S(2)}) async-start(s8[7340032]{0:T(1024)(128)(4,1)} %bitcast.70), calls=%async_computation.12 | async-start | bytes 8388608
  120.0 22.2 %slice-start.14 = ((s8[7340032]{0:T(1024)(128)(4,1)}), s8[4194304]{0:T(1024)(128)(4,1)S(1)}, s32[]{:S(2)}) async-start(s8[7340032]{0:T(1024)(128)(4,1)} %bitcast.78), calls=%async_computation.20 | async-start | bytes 8388608
  127.1 15.2 %slice-start.15 = ((s8[7340032]{0:T(1024)(128)(4,1)}), s8[3145728]{0:T(1024)(128)(4,1)S(1)}, s32[]{:S(2)}) async-start(s8[7340032]{0:T(1024)(128)(4,1)} %bitcast.78), calls=%async_computation.21 | async-start | bytes 6291456
  127.1 26.4 %collective-permute-start.7 = (bf16[384,896]{1,0:T(8,128)(2,1)}, bf16[384,896]{1,0:T(8,128)(2,1)}, u32[]{:S(2)}, u32[]{:S(2)}) collective-permute-start(bf16[384,896]{1,0:T(8,128)(2,1)} %get-tuple-element.34), channel_id=1, source_target_pairs={{0,16},{16,0},{1,17},{17,1},{2,18},{18,2},{3,19},{19,3},{4,20},{20... | collective-permute-start | bytes 2064392 | tf_op jit(solution)/shard_map/ppermute | solution.py:19
  135.4 25.1 %collective-permute-start.8 = (bf16[384,896]{1,0:T(8,128)(2,1)}, bf16[384,896]{1,0:T(8,128)(2,1)}, u32[]{:S(2)}, u32[]{:S(2)}) collective-permute-start(bf16[384,896]{1,0:T(8,128)(2,1)} %get-tuple-element.32), channel_id=1, source_target_pairs={{0,16},{16,0},{1,17},{17,1},{2,18},{18,2},{3,19},{19,3},{4,20},{20... | collective-permute-start | bytes 2064392 | tf_op jit(solution)/shard_map/ppermute | solution.py:19
  142.1 24.5 %collective-permute-start.10 = (bf16[192,4096]{1,0:T(8,128)(2,1)}, bf16[192,4096]{1,0:T(8,128)(2,1)}, u32[]{:S(2)}, u32[]{:S(2)}) collective-permute-start(bf16[192,4096]{1,0:T(8,128)(2,1)} %collective-permute-done.9), channel_id=1, source_target_pairs={{0,4},{4,0},{8,12},{12,8},{1,5},{5,1},{9,13},{13,9},{2,6},{6,2},{1... | collective-permute-start | bytes 4718600 | tf_op jit(solution)/shard_map/ppermute | solution.py:19
  149.2 11.3 %copy-start.16 = (f32[384,896]{1,0:T(8,128)S(1)}, f32[384,896]{1,0:T(8,128)}, u32[]{:S(2)}) copy-start(f32[384,896]{1,0:T(8,128)} %get-tuple-element.35) | copy-start | bytes 4128772
  149.2 11.3 %copy-start.17 = (f32[384,896]{1,0:T(8,128)S(1)}, f32[384,896]{1,0:T(8,128)}, u32[]{:S(2)}) copy-start(f32[384,896]{1,0:T(8,128)} %get-tuple-element.33) | copy-start | bytes 4128772
  149.2 25.5 %collective-permute-start.15 = (bf16[384,896]{1,0:T(8,128)(2,1)}, bf16[384,896]{1,0:T(8,128)(2,1)}, u32[]{:S(2)}, u32[]{:S(2)}) collective-permute-start(bf16[384,896]{1,0:T(8,128)(2,1)} %get-tuple-element.42), channel_id=1, source_target_pairs={{0,16},{16,0},{1,17},{17,1},{2,18},{18,2},{3,19},{19,3},{4,20},{20... | collective-permute-start | bytes 2064392 | tf_op jit(solution)/shard_map/ppermute | solution.py:19
  153.3 85.3 %collective-permute-start.6 = (bf16[192,4096]{1,0:T(8,128)(2,1)}, bf16[192,4096]{1,0:T(8,128)(2,1)}, u32[]{:S(2)}, u32[]{:S(2)}) collective-permute-start(bf16[192,4096]{1,0:T(8,128)(2,1)} %convolution_convert_fusion.1), channel_id=1, source_target_pairs={{0,4},{4,0},{8,12},{12,8},{1,5},{5,1},{9,13},{13,9},{2,6},{6,2},{1... | collective-permute-start | bytes 4718600 | tf_op jit(solution)/shard_map/ppermute | solution.py:19
  173.2 15.3 %collective-permute-start.13 = (bf16[384,896]{1,0:T(8,128)(2,1)S(1)}, bf16[384,896]{1,0:T(8,128)(2,1)S(1)}, u32[]{:S(2)}, u32[]{:S(2)}) collective-permute-start(bf16[384,896]{1,0:T(8,128)(2,1)S(1)} %get-tuple-element.38), channel_id=1, source_target_pairs={{0,16},{16,0},{1,17},{17,1},{2,18},{18,2},{3,19},{19,3},{4,20},{20... | collective-permute-start | bytes 2064392 | tf_op jit(solution)/shard_map/ppermute | solution.py:19
  176.4 12.2 %copy-start.26 = (f32[384,896]{1,0:T(8,128)S(1)}, f32[384,896]{1,0:T(8,128)}, u32[]{:S(2)}) copy-start(f32[384,896]{1,0:T(8,128)} %get-tuple-element.39) | copy-start | bytes 4128772
  179.3 9.4 %copy-start.18 = (f32[384,896]{1,0:T(8,128)S(1)}, f32[384,896]{1,0:T(8,128)}, u32[]{:S(2)}) copy-start(f32[384,896]{1,0:T(8,128)} %get-tuple-element.33) | copy-start | bytes 4128772
  179.3 18.5 %collective-permute-start.11 = (bf16[192,4096]{1,0:T(8,128)(2,1)}, bf16[192,4096]{1,0:T(8,128)(2,1)}, u32[]{:S(2)}, u32[]{:S(2)}) collective-permute-start(bf16[192,4096]{1,0:T(8,128)(2,1)} %convolution_convert_fusion), channel_id=1, source_target_pairs={{0,4},{4,0},{8,12},{12,8},{1,5},{5,1},{9,13},{13,9},{2,6},{6,2},{1... | collective-permute-start | bytes 4718600 | tf_op jit(solution)/shard_map/ppermute | solution.py:19
  190.8 12.1 %copy-start.1 = (bf16[384,896]{1,0:T(8,128)(2,1)}, bf16[384,896]{1,0:T(8,128)(2,1)S(1)}, u32[]{:S(2)}) copy-start(bf16[384,896]{1,0:T(8,128)(2,1)S(1)} %get-tuple-element.31) | copy-start | bytes 2064388
  190.8 13.9 %copy-start.8 = (bf16[384,896]{1,0:T(8,128)(2,1)}, bf16[384,896]{1,0:T(8,128)(2,1)S(1)}, u32[]{:S(2)}) copy-start(bf16[384,896]{1,0:T(8,128)(2,1)S(1)} %get-tuple-element.30) | copy-start | bytes 2064388
  194.8 9.9 %collective-permute-start.14 = (bf16[192,4096]{1,0:T(8,128)(2,1)S(1)}, bf16[192,4096]{1,0:T(8,128)(2,1)S(1)}, u32[]{:S(2)}, u32[]{:S(2)}) collective-permute-start(bf16[192,4096]{1,0:T(8,128)(2,1)S(1)} %fusion), channel_id=1, source_target_pairs={{0,4},{4,0},{8,12},{12,8},{1,5},{5,1},{9,13},{13,9},{2,6},{6,2},{1... | collective-permute-start | bytes 4718600 | tf_op jit(solution)/shard_map/ppermute | solution.py:19
  197.9 10.4 %copy-start.3 = (bf16[384,896]{1,0:T(8,128)(2,1)}, bf16[384,896]{1,0:T(8,128)(2,1)S(1)}, u32[]{:S(2)}) copy-start(bf16[384,896]{1,0:T(8,128)(2,1)S(1)} %get-tuple-element.23) | copy-start | bytes 2064388
  201.4 37.3 %collective-permute-start.12 = (bf16[192,4096]{1,0:T(8,128)(2,1)S(1)}, bf16[192,4096]{1,0:T(8,128)(2,1)S(1)}, u32[]{:S(2)}, u32[]{:S(2)}) collective-permute-start(bf16[192,4096]{1,0:T(8,128)(2,1)S(1)} %add_convert_fusion.3), channel_id=1, source_target_pairs={{0,8},{4,12},{8,0},{12,4},{1,9},{5,13},{9,1},{13,5},{2,10},{6,14},... | collective-permute-start | bytes 4718600 | tf_op jit(solution)/shard_map/ppermute | solution.py:19
  207.7 64.3 %collective-permute-start.17 = (bf16[192,4096]{1,0:T(8,128)(2,1)}, bf16[192,4096]{1,0:T(8,128)(2,1)}, u32[]{:S(2)}, u32[]{:S(2)}) collective-permute-start(bf16[192,4096]{1,0:T(8,128)(2,1)} %add_convert_fusion.2), channel_id=1, source_target_pairs={{0,8},{4,12},{8,0},{12,4},{1,9},{5,13},{9,1},{13,5},{2,10},{6,14},... | collective-permute-start | bytes 4718600 | tf_op jit(solution)/shard_map/ppermute | solution.py:19
  208.3 30.4 %copy-start = (f32[192,4096]{1,0:T(8,128)S(1)}, f32[192,4096]{1,0:T(8,128)}, u32[]{:S(2)}) copy-start(f32[192,4096]{1,0:T(8,128)} %fusion.45) | copy-start | bytes 9437188
  240.7 14.5 %slice-start.2 = ((s8[7340032]{0:T(1024)(128)(4,1)}), s8[3145728]{0:T(1024)(128)(4,1)S(1)}, s32[]{:S(2)}) async-start(s8[7340032]{0:T(1024)(128)(4,1)} %bitcast.66), calls=%async_computation.8 | async-start | bytes 6291456
  242.1 70.8 %reduce-scatter.5.cloned.1.call-start = ((), (), s32[]{:S(2)}) async-start(), calls=%async_computation.3 | async-start | bytes 1966080 | tf_op jit(solution)/shard_map/reduce_scatter | solution.py:57
  242.6 12.6 %slice-start.3 = ((s8[7340032]{0:T(1024)(128)(4,1)}), s8[4194304]{0:T(1024)(128)(4,1)S(1)}, s32[]{:S(2)}) async-start(s8[7340032]{0:T(1024)(128)(4,1)} %bitcast.66), calls=%async_computation.9 | async-start | bytes 8388608
  248.6 23.4 %collective-permute-start.16 = (bf16[192,4096]{1,0:T(8,128)(2,1)S(1)}, bf16[192,4096]{1,0:T(8,128)(2,1)S(1)}, u32[]{:S(2)}, u32[]{:S(2)}) collective-permute-start(bf16[192,4096]{1,0:T(8,128)(2,1)S(1)} %fusion.1), channel_id=1, source_target_pairs={{0,4},{4,0},{8,12},{12,8},{1,5},{5,1},{9,13},{13,9},{2,6},{6,2},{1... | collective-permute-start | bytes 4718600 | tf_op jit(solution)/shard_map/ppermute | solution.py:19
  274.1 13.1 %slice-start.10 = ((s8[6291456]{0:T(1024)(128)(4,1)}), s8[2097152]{0:T(1024)(128)(4,1)S(1)}, s32[]{:S(2)}) async-start(s8[6291456]{0:T(1024)(128)(4,1)} %bitcast.74), calls=%async_computation.16 | async-start | bytes 4194304
  275.9 11.3 %slice-start.11 = ((s8[6291456]{0:T(1024)(128)(4,1)}), s8[4194304]{0:T(1024)(128)(4,1)S(1)}, s32[]{:S(2)}) async-start(s8[6291456]{0:T(1024)(128)(4,1)} %bitcast.74), calls=%async_computation.17 | async-start | bytes 8388608
  275.9 11.3 %copy-start.2 = (bf16[384,896]{1,0:T(8,128)(2,1)S(1)}, bf16[384,896]{1,0:T(8,128)(2,1)}, u32[]{:S(2)}) copy-start(bf16[384,896]{1,0:T(8,128)(2,1)} %copy-done.1) | copy-start | bytes 2064388
  275.9 11.3 %copy-start.5 = (bf16[384,896]{1,0:T(8,128)(2,1)S(1)}, bf16[384,896]{1,0:T(8,128)(2,1)}, u32[]{:S(2)}) copy-start(bf16[384,896]{1,0:T(8,128)(2,1)} %copy-done.3) | copy-start | bytes 2064388
  275.9 20.6 %slice-start.12 = ((s8[6291456]{0:T(1024)(128)(4,1)}), s8[4194304]{0:T(1024)(128)(4,1)S(1)}, s32[]{:S(2)}) async-start(s8[6291456]{0:T(1024)(128)(4,1)} %bitcast.76), calls=%async_computation.18 | async-start | bytes 8388608
  296.6 9.5 %copy-start.21 = (f32[1024,192]{0,1:T(8,128)S(1)}, f32[1024,192]{0,1:T(8,128)}, u32[]{:S(2)}) copy-start(f32[1024,192]{0,1:T(8,128)} %param.8) | copy-start | bytes 2359300
  296.6 16.3 %copy-start.23 = (f32[1024,192]{0,1:T(8,128)S(1)}, f32[1024,192]{0,1:T(8,128)}, u32[]{:S(2)}) copy-start(f32[1024,192]{0,1:T(8,128)} %param.9) | copy-start | bytes 2359300
  (18 other events, 93.4 us)
Sparse Core Ops, SparseCore 0:
  10.1 39.7 all-gather.4
  54.5 36.0 all-gather.6
  242.2 34.1 reduce-scatter.2
  278.6 34.2 reduce-scatter.4
